TPU v7x, 32 devices: a whole 2x2x4 slice. The times are simulated.
32 devices in a mesh: dp: 8 (over z, y), mp: 4 (over x, core).
Axes of the slice: x: 2, y: 2, z: 4, core: 2. Of those that a mesh axis runs over, the one named last changes fastest.
Arguments:
- tokens: bfloat16 [2048, 4096], P('dp', 'mp'), may hold values from -24 to 24
- cotangent: bfloat16 [2048, 4096], P('dp', 'mp'), may hold values from -6 to 6
- gain_dec: float32 [4096], replicated, may hold values from 0.1 to 1.9
- w_query: bfloat16 [4096, 4096], P(None, 'mp'), may hold values from -1 to 1
- w_out: bfloat16 [4096, 4096], P('mp'), may hold values from -0.5 to 0.5
- encodings: bfloat16 [64, 128, 896], P('dp', 'mp'), may hold values from -24 to 24
- gain_enc: float32 [896], replicated, may hold values from 0.1 to 1.9
- w_key: bfloat16 [896, 4096], P(None, 'mp'), may hold values from -1 to 1
- w_value: bfloat16 [896, 4096], P(None, 'mp'), may hold values from -0.1875 to 0.1875
- gain_post: float32 [4096], replicated, may hold values from 0.1 to 1.9
- neighbour_ids: int32 [32, 2], P('dp'), may hold values from 0 to 63, as said below
Outputs:
- mixed: bfloat16 [2048, 4096], P('dp', 'mp')
- ffn_input: bfloat16 [2048, 4096], P('dp', 'mp')
- d_encodings: bfloat16 [64, 128, 896], P('dp', 'mp')
Inputs may be any that keep to these rules, and one draw needn't show every extreme that they name: `neighbour_ids`: encoder row g is held by index g // 8 of dp. Every encoder row is retrieved by exactly one block. The blocks of one index of dp retrieve at most 1 row held by any one index of dp, and exactly 1 from some.
All inputs are finite; a program needn't handle non-finite values.
Results may differ from a plain program's by a relative error of at most 0.02.
The roundings to bfloat16 on the way count: a program that leaves them out, or rounds other values in their place, can miss the bound.
Values may be sent and summed in bfloat16 or wider, within the bound.
A program may use at most 64 MiB of HBM per device.

v0:
```python
import jax
import jax.numpy as jnp
from jax import lax
from jax.sharding import PartitionSpec as P

HD = 128
BLOCK = 64
NLEN = 128
NEIGH = 2


EPS = 1e-06


def rms_scale(values):
    return lax.rsqrt(jnp.mean(values * values, axis=-1, keepdims=True) + EPS)


def shards(
    tokens,
    cotangent,
    gain_dec,
    w_query,
    w_out,
    encodings,
    gain_enc,
    w_key,
    w_value,
    gain_post,
    neighbour_ids,
):
    dp_count = lax.axis_size("dp")
    seq_len = tokens.shape[0]
    share_cols = tokens.shape[1]
    head_cols = w_query.shape[1]
    heads_here = head_cols // HD
    own_rows = encodings.shape[0]
    blocks = neighbour_ids.shape[0]
    readings = blocks * neighbour_ids.shape[1]
    per_holder = (readings + dp_count - 1) // dp_count
    slot_count = dp_count * per_holder
    lead_in = BLOCK - 1
    score_scale = HD ** (-0.5)
    whole_x, whole_dy = (
        lax.all_gather(tokens, "mp", axis=1, tiled=True),
        lax.all_gather(cotangent, "mp", axis=1, tiled=True),
    )
    tok_wide = whole_x.astype(jnp.float32)
    normed = (tok_wide * rms_scale(tok_wide) * gain_dec).astype(jnp.bfloat16)
    queries = jnp.dot(normed, w_query, preferred_element_type=jnp.float32).astype(jnp.bfloat16)
    chosen = neighbour_ids.reshape(readings)
    owner_of = chosen // own_rows
    local_row = chosen % own_rows
    positions = jnp.arange(readings, dtype=jnp.int32)
    same_owner = owner_of[:, None] == owner_of[None, :]
    earlier = (chosen[None, :] < chosen[:, None]) | (chosen[None, :] == chosen[:, None]) & (
        positions[None, :] < positions[:, None]
    )
    slot_rank = jnp.sum((same_owner & earlier).astype(jnp.int32), axis=1)
    slot_of = owner_of * per_holder + slot_rank
    slot_ids = jnp.arange(slot_count, dtype=jnp.int32)
    matches = slot_of[:, None] == slot_ids[None, :]
    wanted = jnp.sum(jnp.where(matches, local_row[:, None] + 1, 0), axis=0) - 1
    requested = lax.all_to_all(
        wanted.reshape(dp_count, per_holder), "dp", split_axis=0, concat_axis=0, tiled=True
    ).reshape(slot_count)
    enc_wide = encodings.astype(jnp.float32)
    row_scale = rms_scale(enc_wide)
    normed_enc = (enc_wide * row_scale * gain_enc).astype(jnp.bfloat16)
    select = requested[:, None] == jnp.arange(own_rows, dtype=jnp.int32)[None, :]
    outgoing = jnp.einsum(
        "sj,jte->ste", select.astype(jnp.bfloat16), normed_enc, preferred_element_type=jnp.float32
    ).astype(jnp.bfloat16)
    incoming = lax.all_to_all(outgoing, "dp", split_axis=0, concat_axis=0, tiled=True)
    picked = jnp.einsum(
        "as,ste->ate", matches.astype(jnp.bfloat16), incoming, preferred_element_type=jnp.float32
    ).astype(jnp.bfloat16)
    w_both = jnp.concatenate([w_key, w_value], axis=1)
    key_values = jnp.einsum(
        "ate,ej->atj",
        lax.all_gather(picked, "mp", axis=1, tiled=True),
        w_both,
        preferred_element_type=jnp.float32,
    ).astype(jnp.bfloat16)
    key_blocks = key_values[..., :head_cols].reshape(blocks, NEIGH * NLEN, heads_here, HD)
    value_blocks = key_values[..., head_cols:].reshape(blocks, NEIGH * NLEN, heads_here, HD)
    pad_rows = jnp.zeros((lead_in, head_cols), jnp.bfloat16)
    shifted = jnp.concatenate([queries[lead_in:], pad_rows], axis=0).reshape(
        blocks, BLOCK, heads_here, HD
    )
    scores = (
        jnp.einsum("cqhd,ckhd->chqk", shifted, key_blocks, preferred_element_type=jnp.float32)
        * score_scale
    )
    row_max = jnp.max(scores, axis=-1, keepdims=True)
    lifted = jnp.exp(scores - row_max)
    probability = lifted / jnp.sum(lifted, axis=-1, keepdims=True)
    weights = probability.astype(jnp.bfloat16)
    attended = jnp.einsum(
        "chqk,ckhd->cqhd", weights, value_blocks, preferred_element_type=jnp.float32
    ).astype(jnp.bfloat16)
    attended = jnp.concatenate(
        [pad_rows, attended.reshape(seq_len, head_cols)[: seq_len - lead_in]], axis=0
    )
    branch = jnp.dot(attended, w_out, preferred_element_type=jnp.float32)
    column0 = lax.axis_index("mp") * share_cols
    summed = lax.psum(branch.astype(jnp.bfloat16), "mp").astype(jnp.float32)
    mixed_full = (tok_wide + summed).astype(jnp.bfloat16)
    mixed_wide = mixed_full.astype(jnp.float32)
    ffn_full = (mixed_wide * rms_scale(mixed_wide) * gain_post).astype(jnp.bfloat16)
    mixed_out = lax.dynamic_slice_in_dim(mixed_full, column0, share_cols, 1)
    ffn_out = lax.dynamic_slice_in_dim(ffn_full, column0, share_cols, 1)
    d_attended = lax.dot_general(
        whole_dy, w_out, (((1,), (1,)), ((), ())), preferred_element_type=jnp.float32
    ).astype(jnp.bfloat16)
    d_shifted = jnp.concatenate([d_attended[lead_in:], pad_rows], axis=0).reshape(
        blocks, BLOCK, heads_here, HD
    )
    value_grad = jnp.einsum(
        "chqk,cqhd->ckhd", weights, d_shifted, preferred_element_type=jnp.float32
    ).astype(jnp.bfloat16)
    d_probability = jnp.einsum(
        "cqhd,ckhd->chqk", d_shifted, value_blocks, preferred_element_type=jnp.float32
    )
    d_scores = (
        probability
        * (d_probability - jnp.sum(probability * d_probability, axis=-1, keepdims=True))
        * score_scale
    ).astype(jnp.bfloat16)
    key_grad = jnp.einsum(
        "chqk,cqhd->ckhd", d_scores, shifted, preferred_element_type=jnp.float32
    ).astype(jnp.bfloat16)
    both_grads = jnp.concatenate(
        [
            key_grad.reshape(readings, NLEN, head_cols),
            value_grad.reshape(readings, NLEN, head_cols),
        ],
        axis=2,
    )
    d_normed = lax.psum_scatter(
        jnp.einsum("atj,ej->tae", both_grads, w_both, preferred_element_type=jnp.float32).astype(
            jnp.bfloat16
        ),
        "mp",
        scatter_dimension=0,
        tiled=True,
    ).astype(jnp.float32)
    back_out = jnp.einsum(
        "as,tae->ste", matches.astype(jnp.float32), d_normed, precision=lax.Precision.HIGHEST
    )
    back_in = lax.all_to_all(back_out, "dp", split_axis=0, concat_axis=0, tiled=True)
    grad_rows = jnp.einsum(
        "sj,ste->jte", select.astype(jnp.float32), back_in, precision=lax.Precision.HIGHEST
    )
    enc_hat = enc_wide * row_scale
    upstream = gain_enc * grad_rows
    d_encodings = (
        row_scale * (upstream - enc_hat * jnp.mean(upstream * enc_hat, axis=-1, keepdims=True))
    ).astype(jnp.bfloat16)
    return (mixed_out, ffn_out, d_encodings)


def solution(mesh):
    in_specs = (
        P("dp", "mp"),
        P("dp", "mp"),
        P(),
        P(None, "mp"),
        P("mp", None),
        P("dp", "mp", None),
        P(),
        P(None, "mp"),
        P(None, "mp"),
        P(),
        P("dp", None),
    )
    out_specs = (P("dp", "mp"), P("dp", "mp"), P("dp", "mp", None))
    return jax.shard_map(shards, mesh=mesh, in_specs=in_specs, out_specs=out_specs, check_vma=False)
```

profile of v0, /device:TPU:0, one launch (start us, length us, event | category | flops | bytes accessed | tf_op | source)
XLA Modules:
  0.0 246.2 jit_solution(6428867362311420894)
XLA Ops:
  7.2 0.7 all-gather.8.cloned.1.call-update
  7.9 0.7 all-gather.4.cloned.1.call-update
  8.6 0.8 copy.99
  9.5 0.2 convert_reduce_fusion
  9.8 0.7 copy.100
  10.5 7.3 %all-to-all-start = ((s32[8,1,1]{2,1,0:T(1,128)}), s32[8,1,1]{2,1,0:T(1,128)S(1)}, u32[]{:S(2)}, u32[]{:S(2)}) async-start(s32[8,1,1]{2,1,0:T(1,128)} %copy.100), calls=%async_computation | async-start | bytes 8192 | tf_op jit(solution)/shard_map/all_to_all | solution.py:64
  17.8 1.3 fusion.47
  19.1 5.1 %all-to-all-done = s32[8,1,1]{2,1,0:T(1,128)S(1)} async-done(((s32[8,1,1]{2,1,0:T(1,128)}), s32[8,1,1]{2,1,0:T(1,128)S(1)}, u32[]{:S(2)}, u32[]{:S(2)}) %all-to-all-start) | async-done | bytes 64 | tf_op jit(solution)/shard_map/all_to_all | solution.py:64
  24.2 0.2 reduce
  24.4 1.4 convolution_convert_fusion.3
  25.9 14.4 %all_to_all.16 = bf16[8,32,896]{2,1,0:T(8,128)(2,1)S(1)} all-to-all(bf16[8,32,896]{2,1,0:T(8,128)(2,1)S(1)} %copy.103), channel_id=1, replica_groups=mesh['dp'=8,'mp'=4] {'dp'}, dimensions={0} | all-to-all | bytes 917504 | tf_op jit(solution)/shard_map/all_to_all | solution.py:74
  40.3 1.1 convolution_convert_fusion.2
  41.5 7.0 %fusion.93 = bf16[256,1024]{1,0:T(8,128)(2,1)S(1)} fusion(bf16[256,4096]{1,0:T(8,128)(2,1)} %all-gather.8.cloned.1.call-done, bf16[1024,4096]{1,0:T(8,128)(2,1)} %param.15), kind=kOutput, calls=%fused_computation.110 | convolution fusion | flops 2147483648 | bytes 11010048 | tf_op jit(solution)/shard_map/dot_general | solution.py:113
  48.8 10.2 %all-gather.4.cloned.1.call-done = bf16[256,4096]{1,0:T(8,128)(2,1)} async-done(((bf16[256,1024]{1,0:T(8,128)(2,1)}), bf16[256,4096]{1,0:T(8,128)(2,1)}) %all-gather.4.cloned.1.call-update) | async-done | bytes 2097168 | tf_op jit(solution)/shard_map/all_gather | solution.py:45
  59.1 2.2 fusion.2
  61.3 5.7 %fusion.10 = bf16[256,1024]{1,0:T(8,128)(2,1)S(1)} fusion(bf16[4096,1024]{1,0:T(8,128)(2,1)} %param.14, bf16[256,4096]{1,0:T(8,128)(2,1)S(1)} %copy-done, f32[4096]{0:T(1024)S(1)} %copy-done.5, f32[256]{0:T(256)S(1)} %add_rsqrt_fusion.2), kind=kOutput, calls=%fused_computation.17 | convolution fusion | flops 2151677952 | bytes 11027456 | tf_op jit(solution)/shard_map/dot_general | solution.py:50
  67.4 15.0 %all-gather.6.cloned.1.call-done = bf16[8,128,896]{2,0,1:T(8,128)(2,1)} async-done(((bf16[8,32,896]{2,0,1:T(8,128)(2,1)}), bf16[8,128,896]{2,0,1:T(8,128)(2,1)}) %all-gather.6.cloned.1.call-update) | async-done | bytes 1835024 | tf_op jit(solution)/shard_map/all_gather | solution.py:81
  82.4 7.1 %convolution_convert_fusion.1 = bf16[8,128,2048]{2,1,0:T(8,128)(2,1)S(1)} fusion(bf16[896,1024]{1,0:T(8,128)(2,1)} %param.19, bf16[896,1024]{1,0:T(8,128)(2,1)} %param.18, bf16[8,128,896]{2,0,1:T(8,128)(2,1)} %all-gather.6.cloned.1.call-done), kind=kOutput, calls=%fused_computation.15 | convolution fusion | flops 3767533568 | bytes 9699328 | tf_op jit(solution)/shard_map/ate,ej->atj/dot_general | solution.py:79
  89.5 0.4 fusion.91
  89.9 0.6 copy.126
  90.5 0.6 copy.127
  91.2 0.8 fusion.12
  92.0 2.0 fusion.92
  94.1 2.2 fusion.20
  96.3 7.1 %convert_bitcast_fusion = bf16[4,256,8,128]{1,3,2,0:T(8,128)(2,1)} fusion(bf16[4,64,8,128]{3,2,1,0:T(8,128)(2,1)S(1)} %bitcast.64, f32[4,8,64]{2,1,0:T(8,128)S(1)} %get-tuple-element.27, f32[4,8,64,256]{3,2,1,0:T(8,128)} %copy-done.2), kind=kOutput, calls=%fused_computation.20 | convolution fusion | flops 137365760 | bytes 4726784 | tf_op jit(solution)/shard_map/chqk,cqhd->ckhd/dot_general | solution.py:119
  103.4 16.5 %convert_bitcast_fusion.1 = bf16[4,256,8,128]{1,3,2,0:T(8,128)(2,1)} fusion(f32[4,8,64,256]{3,2,1,0:T(8,128)} %fusion.20, bf16[4,64,8,128]{3,2,1,0:T(8,128)(2,1)S(1)} %bitcast.66, f32[4,8,64,256]{3,2,1,0:T(8,128)} %get-tuple-element.28, f32[4,8,64]{2,1,0:T(8,128)S(1)} %get-tuple-element.27), kind=kOutput, calls=%fused_computation.21 | convolution fusion | flops 138938624 | bytes 6823936 | tf_op jit(solution)/shard_map/chqk,cqhd->ckhd/dot_general | solution.py:130
  119.9 4.3 %copy.114 = bf16[4,256,8,128]{3,2,1,0:T(8,128)(2,1)} copy(bf16[4,256,8,128]{1,3,2,0:T(8,128)(2,1)} %convert_bitcast_fusion.1) | data formatting | bytes 4194304 | tf_op jit(solution)/shard_map/convert_element_type | solution.py:132
  124.2 4.2 %reshape.177 = bf16[8,128,1024]{2,1,0:T(8,128)(2,1)} reshape(bf16[4,256,8,128]{3,2,1,0:T(8,128)(2,1)} %copy.114) | data formatting | bytes 4194304 | tf_op jit(solution)/shard_map/reshape | solution.py:135
  128.4 4.3 %copy.116 = bf16[4,256,8,128]{3,2,1,0:T(8,128)(2,1)} copy(bf16[4,256,8,128]{1,3,2,0:T(8,128)(2,1)} %convert_bitcast_fusion) | data formatting | bytes 4194304 | tf_op jit(solution)/shard_map/convert_element_type | solution.py:121
  132.7 4.2 %reshape.178 = bf16[8,128,1024]{2,1,0:T(8,128)(2,1)} reshape(bf16[4,256,8,128]{3,2,1,0:T(8,128)(2,1)} %copy.116) | data formatting | bytes 4194304 | tf_op jit(solution)/shard_map/reshape | solution.py:136
  136.9 7.8 %convert_bitcast_fusion.2 = bf16[128,8,896]{0,2,1:T(8,128)(2,1)} fusion(bf16[8,128,1024]{2,1,0:T(8,128)(2,1)} %reshape.178, bf16[8,128,1024]{2,1,0:T(8,128)(2,1)} %reshape.177, bf16[896,1024]{1,0:T(8,128)(2,1)} %param.19, bf16[896,1024]{1,0:T(8,128)(2,1)} %param.18), kind=kOutput, calls=%fused_computation.35 | convolution fusion | flops 3774742528 | bytes 9699328 | tf_op jit(solution)/shard_map/atj,ej->tae/dot_general | solution.py:141
  144.7 3.9 %copy.117 = bf16[128,8,896]{2,1,0:T(8,128)(2,1)} copy(bf16[128,8,896]{0,2,1:T(8,128)(2,1)} %convert_bitcast_fusion.2) | data formatting | bytes 3670016 | tf_op jit(solution)/shard_map/convert_element_type | solution.py:141
  148.6 0.3 all-reduce.5.cloned.1.call-start
  148.9 5.9 %fusion.32 = bf16[4,64,8,128]{3,1,2,0:T(8,128)(2,1)S(1)} fusion(bf16[4,256,8,128]{3,2,1,0:T(8,128)(2,1)} %bitcast.59, f32[4,8,64]{2,1,0:T(8,128)S(1)} %get-tuple-element.27, f32[4,8,64,256]{3,2,1,0:T(8,128)} %copy-done.2), kind=kOutput, calls=%fused_computation.40 | convolution fusion | flops 136579328 | bytes 4726784 | tf_op jit(solution)/shard_map/chqk,ckhd->cqhd/dot_general | solution.py:99
  154.8 0.3 copy.110
  155.3 7.6 %convolution_convert_fusion = bf16[256,4096]{1,0:T(8,128)(2,1)} fusion(bf16[1024,4096]{1,0:T(8,128)(2,1)} %param.15, bf16[193,1024]{1,0:T(8,128)(2,1)S(1)} %slice.23), kind=kOutput, calls=%fused_computation.5 | convolution fusion | flops 2148532224 | bytes 10881024 | tf_op jit(solution)/shard_map/dot_general | solution.py:105
  162.9 15.7 %reduce-scatter.2.cloned.1.call-done = bf16[32,8,896]{2,1,0:T(8,128)(2,1)} async-done(((bf16[128,8,896]{2,1,0:T(8,128)(2,1)}), bf16[32,8,896]{2,1,0:T(8,128)(2,1)}) %reduce-scatter.2.cloned.1.call-update) | async-done | bytes 458768 | tf_op jit(solution)/shard_map/reduce_scatter | solution.py:140
  178.6 1.3 fusion.62
  179.9 1.1 copy.118
  181.0 5.5 %all-to-all-start.2 = ((f32[8,32,896]{2,1,0:T(8,128)}), f32[8,32,896]{2,1,0:T(8,128)S(1)}, u32[]{:S(2)}, u32[]{:S(2)}) async-start(f32[8,32,896]{2,1,0:T(8,128)} %copy.118), calls=%async_computation.3 | async-start | bytes 1835008 | tf_op jit(solution)/shard_map/all_to_all | solution.py:151
  186.5 45.8 %all-reduce.5.cloned.1.call-done = bf16[256,4096]{1,0:T(8,128)(2,1)} async-done(((bf16[256,4096]{1,0:T(8,128)(2,1)}), bf16[256,4096]{1,0:T(8,128)(2,1)}) %all-reduce.5.cloned.1.call-update) | async-done | bytes 2097168 | tf_op jit(solution)/shard_map/psum | solution.py:107
  232.3 2.5 %multiply_reduce_fusion = (f32[256]{0:T(256)S(1)}, bf16[256,4096]{1,0:T(8,128)(2,1)S(1)}) fusion(bf16[256,4096]{1,0:T(8,128)(2,1)} %all-reduce.5.cloned.1.call-done, bf16[256,4096]{1,0:T(8,128)(2,1)S(1)} %copy-done), kind=kLoop, calls=%fused_computation.14 | loop fusion | flops 7339776 | bytes 6292480 | tf_op jit(solution)/shard_map/reduce_sum | solution.py:16
  234.9 0.5 convert_element_type.98
  235.4 0.8 constant_dynamic-slice_fusion
  236.3 1.0 fusion.39
  237.2 1.3 fusion.43
  238.5 0.3 fusion.46
  238.8 0.8 copy.120
  (41 shorter events, 1.2 us)
Async XLA Ops:
  7.2 34.3 %all-gather.8.cloned.1.call-start = ((), (), s32[]{:S(2)}) async-start(), calls=%async_computation.7 | async-start | bytes 2621440 | tf_op jit(solution)/shard_map/all_gather | solution.py:46
  7.9 51.2 %all-gather.4.cloned.1.call-start = ((), (), s32[]{:S(2)}) async-start(), calls=%async_computation.4 | async-start | bytes 2621440 | tf_op jit(solution)/shard_map/all_gather | solution.py:45
  10.5 13.7 %all-to-all-start = ((s32[8,1,1]{2,1,0:T(1,128)}), s32[8,1,1]{2,1,0:T(1,128)S(1)}, u32[]{:S(2)}, u32[]{:S(2)}) async-start(s32[8,1,1]{2,1,0:T(1,128)} %copy.100), calls=%async_computation | async-start | bytes 8192 | tf_op jit(solution)/shard_map/all_to_all | solution.py:64
  17.8 64.6 %all-gather.6.cloned.1.call-start = ((), (), s32[]{:S(2)}) async-start(), calls=%async_computation.5 | async-start | bytes 2293760 | tf_op jit(solution)/shard_map/all_gather | solution.py:81
  41.4 137.2 %reduce-scatter.2.cloned.1.call-start = ((), (), s32[]{:S(2)}) async-start(), calls=%async_computation.8 | async-start | bytes 2293760 | tf_op jit(solution)/shard_map/reduce_scatter | solution.py:140
  48.7 12.6 %copy-start.5 = (f32[4096]{0:T(1024)S(1)}, f32[4096]{0:T(1024)}, u32[]{:S(2)}) copy-start(f32[4096]{0:T(1024)} %param.13) | copy-start | bytes 49156
  59.1 2.3 copy-start
  91.2 2.9 %copy-start.1 = (bf16[128,8,8,128]{3,2,1,0:T(8,128)(2,1)}, bf16[128,8,8,128]{3,2,1,0:T(8,128)(2,1)S(1)}, u32[]{:S(2)}) copy-start(bf16[128,8,8,128]{3,2,1,0:T(8,128)(2,1)S(1)} %copy.127) | copy-start | bytes 6291460
  92.0 2.0 copy-start.2
  148.6 83.7 %all-reduce.5.cloned.1.call-start = ((), (), s32[]{:S(2)}) async-start(), calls=%async_computation.6 | async-start | bytes 4194304 | tf_op jit(solution)/shard_map/psum | solution.py:107
  181.0 56.2 %all-to-all-start.2 = ((f32[8,32,896]{2,1,0:T(8,128)}), f32[8,32,896]{2,1,0:T(8,128)S(1)}, u32[]{:S(2)}, u32[]{:S(2)}) async-start(f32[8,32,896]{2,1,0:T(8,128)} %copy.118), calls=%async_computation.3 | async-start | bytes 1835008 | tf_op jit(solution)/shard_map/all_to_all | solution.py:151
  234.9 1.4 dynamic-slice-start
  235.4 1.8 copy-start.3
  235.4 1.8 copy-start.4
Sparse Core Ops, SparseCore 0:
  9.6 25.2 all-gather.7
  36.4 22.5 all-gather.3
  61.2 21.1 all-gather.5
  148.8 29.7 reduce-scatter.1
  180.9 51.3 all-reduce.4
where the time goes:
time: 247 us; the launch traced here: 246 us
  waiting for transfers between devices  93.3 us (38%)
  matrix products  72.9 us (30%)
  local copies, waits for them, and re-layouts  27.9 us (11%)
  blocking collectives  14.4 us (6%)
  between operations  14 us (6%)
  starting transfers between devices  13.2 us (5%)
  other arithmetic  10.3 us (4%)
    psum x1, waiting for transfers between devices, shards(): summed = lax.psum(branch.astype(jnp.bfloat16), 'mp').astype(jnp.float32)  45.8 us
    dot_general x1, matrix products, shards(): jnp.einsum('chqk,cqhd->ckhd', d_scores, shifted, preferred_element_type=j...  16.5 us
    reduce_scatter x1, waiting for transfers between devices, shards(): lax.psum_scatter(jnp.einsum('atj,ej->tae', both_grads, w_both, preferred_...  15.7 us
    all_gather x1, waiting for transfers between devices, shards(): lax.all_gather(picked, 'mp', axis=1, tiled=True)  15 us
    all_to_all x1, blocking collectives, shards(): lax.all_to_all(outgoing, 'dp', split_axis=0, concat_axis=0, tiled=True)  14.4 us
    all_gather x1, waiting for transfers between devices, shards(): lax.all_gather(tokens, 'mp', axis=1, tiled=True)  10.2 us
    dot_general x1, matrix products, shards(): jnp.einsum('atj,ej->tae', both_grads, w_both, preferred_element_type=jnp....  7.84 us
    dot_general x1, matrix products, shards(): branch = jnp.dot(attended, w_out, preferred_element_type=jnp.float32)  7.61 us
  transfers between devices with their start and end apart: 7, of which 5 were waited for; matrix products, arithmetic and copies ran while one was open for 17% of the time, Pallas kernels for 0%

commit v1 on v0

v1 whole, which is shorter than its diff:
```python
import functools

import jax
import jax.numpy as jnp
from jax import lax
from jax.experimental import pallas as pl
from jax.experimental.pallas import tpu as pltpu
from jax.sharding import PartitionSpec as P

HD = 128
BLOCK = 64
NLEN = 128
NEIGH = 2
LEAD = BLOCK - 1
EPS = 1e-06
MESH = pl.DeviceIdType.MESH
BF16 = jnp.bfloat16
F32 = jnp.float32
NT = (((1,), (1,)), ((), ()))
TN = (((0,), (0,)), ((), ()))


def rms_scale(values):
    return lax.rsqrt(jnp.mean(values * values, axis=-1, keepdims=True) + EPS)


def place(n_dp, n_mp):
    d, m = lax.axis_index("dp"), lax.axis_index("mp")
    n_x = n_mp // 2
    x, c = m // 2, m % 2
    return d, m, n_x, x, c, x * 2 + (1 - c)


def greet(n_dp, n_mp, d, m):
    barrier = pltpu.get_barrier_semaphore()
    for s in range(1, n_dp):
        pl.semaphore_signal(barrier, inc=1, device_id=((d + s) % n_dp, m), device_id_type=MESH)
    for s in range(1, n_mp):
        pl.semaphore_signal(barrier, inc=1, device_id=(d, (m + s) % n_mp), device_id_type=MESH)
    pl.semaphore_wait(barrier, n_dp + n_mp - 2)


def gather_kernel(
    n_dp, n_mp,
    tok, cot, gain_dec, wq_hbm, wo_hbm, enc, gain_enc, wk_hbm, wv_hbm, ids, owner,
    q_out, da_out, k_out, v_out, idtab,
    tok_all, cot_all, enc_all, normed, wq, wo, wk, wv, enc_norm, sending, arrived,
    w_sem, ag_send, ag_recv, id_send, id_recv, row_send, row_recv,
):
    d, m, n_x, x, c, partner = place(n_dp, n_mp)
    own_rows, share, width = enc.shape
    readings = ids.shape[0]
    seq_len, feat = tok.shape
    head_cols = wq.shape[2]
    loads = [
        pltpu.make_async_copy(a, b, w_sem.at[i])
        for i, (a, b) in enumerate([(wq_hbm, wq), (wo_hbm, wo), (wk_hbm, wk), (wv_hbm, wv)])
    ]
    for load in loads:
        load.start()

    def hop(buf, t, kind, chunk, target):
        return pltpu.make_async_remote_copy(
            src_ref=buf.at[chunk], dst_ref=buf.at[chunk],
            send_sem=ag_send.at[t, kind], recv_sem=ag_recv.at[t, kind],
            device_id=(d, target), device_id_type=MESH,
        )

    def spread(buf, t):
        for o in range(1, n_x):
            hop(buf, t, o, m, ((x + o) % n_x) * 2 + c).start()
        hop(buf, t, 0, m, partner).start()

    def forward(buf, t):
        for o in range(1, n_x):
            chunk = ((x + n_x - o) % n_x) * 2 + c
            hop(buf, t, o, chunk, partner).wait_recv()
            hop(buf, t, n_x + o, chunk, partner).start()

    def finish(buf, t):
        hop(buf, t, 0, partner, partner).wait_recv()
        for o in range(1, n_x):
            hop(buf, t, n_x + o, ((x + n_x - o) % n_x) * 2 + 1 - c, partner).wait_recv()

    def sent_far(buf, t):
        for o in range(1, n_x):
            hop(buf, t, o, m, partner).wait_send()

    def sent_near(buf, t):
        hop(buf, t, 0, m, partner).wait_send()
        for o in range(1, n_x):
            hop(buf, t, n_x + o, m, partner).wait_send()

    def id_copy(s, to):
        return pltpu.make_async_remote_copy(
            src_ref=ids, dst_ref=idtab.at[to], send_sem=id_send.at[s], recv_sem=id_recv.at[s],
            device_id=((d + s) % n_dp, m), device_id_type=MESH,
        )

    def row_copy(s, src, dst):
        return pltpu.make_async_remote_copy(
            src_ref=sending.at[src], dst_ref=arrived.at[dst],
            send_sem=row_send.at[s], recv_sem=row_recv.at[s],
            device_id=((d + s) % n_dp, m), device_id_type=MESH,
        )

    tok_all[m] = tok[...]
    greet(n_dp, n_mp, d, m)
    for s in range(1, n_dp):
        id_copy(s, d).start()
    spread(tok_all, 0)
    idtab[d] = ids[...]
    cot_all[m] = cot[...]
    wide = enc[...].astype(F32)
    enc_norm[...] = wide * rms_scale(wide) * gain_enc[...][None]

    def choose(reader):
        asked = idtab[reader]
        total = jnp.zeros((share, width), F32)
        for row in range(own_rows):
            hit = jnp.where(asked == d * own_rows + row, 1.0, 0.0).astype(F32)
            hit = jnp.max(hit, axis=0, keepdims=True)
            total = total + enc_norm[row] * jnp.concatenate([hit] * (width // 128), axis=1)
        return total.astype(BF16)

    arrived[d] = choose(d)
    for s in range(1, n_dp):
        reader = (d + s) % n_dp
        id_copy(n_dp - s, reader).wait_recv()
        sending[reader] = choose(reader)
        row_copy(s, reader, d).start()
    sent_far(tok_all, 0)
    spread(cot_all, 1)
    forward(tok_all, 0)
    for s in range(1, n_dp):
        holder = (d + n_dp - s) % n_dp
        row_copy(s, holder, holder).wait_recv()
    for a in range(readings):
        enc_all[m, a] = arrived[owner[a]]
    spread(enc_all, 2)
    finish(tok_all, 0)
    squares = jnp.zeros((seq_len, 1), F32)
    for k in range(n_mp):
        part = tok_all[k].astype(F32)
        squares = squares + jnp.sum(part * part, axis=-1, keepdims=True)
    scale = lax.rsqrt(squares / (feat * n_mp) + EPS)
    for k in range(n_mp):
        normed[k] = (tok_all[k].astype(F32) * scale * gain_dec[k]).astype(BF16)
    loads[0].wait()
    keep = lax.broadcasted_iota(jnp.int32, (seq_len, 256), 0) < seq_len - LEAD

    def shift_up(values):
        return jnp.where(keep, pltpu.roll(values, seq_len - LEAD, 0), 0.0).astype(BF16)

    def query_tile(n, _):
        cols = pl.ds(pl.multiple_of(n * 256, 256), 256)
        acc = jnp.zeros((seq_len, 256), F32)
        for k in range(n_mp):
            acc += jnp.dot(normed[k], wq[k, :, cols], preferred_element_type=F32)
        q_out[:, cols] = shift_up(acc)
        return 0

    lax.fori_loop(0, head_cols // 256, query_tile, 0)
    forward(cot_all, 1)
    finish(cot_all, 1)
    loads[1].wait()

    def grad_tile(n, _):
        cols = pl.ds(pl.multiple_of(n * 256, 256), 256)
        acc = jnp.zeros((seq_len, 256), F32)
        for k in range(n_mp):
            acc += lax.dot_general(
                cot_all[k], wo[cols, k * feat : (k + 1) * feat], NT, preferred_element_type=F32
            )
        da_out[:, cols] = shift_up(acc)
        return 0

    lax.fori_loop(0, head_cols // 256, grad_tile, 0)
    forward(enc_all, 2)
    finish(enc_all, 2)
    loads[2].wait()
    loads[3].wait()

    def memory_tile(n, _):
        cols = pl.ds(pl.multiple_of(n * 256, 256), 256)
        for k in range(n_mp):
            rows = enc_all[k].reshape(readings * share, width)
            for weight, out in ((wk, k_out), (wv, v_out)):
                part = jnp.dot(rows, weight[:, cols], preferred_element_type=F32).astype(BF16)
                out[:, k * share : (k + 1) * share, cols] = part.reshape(readings, share, 256)
        return 0

    lax.fori_loop(0, head_cols // 256, memory_tile, 0)
    for s in range(1, n_dp):
        id_copy(s, d).wait_send()
        row_copy(s, (d + s) % n_dp, d).wait_send()
    sent_far(cot_all, 1)
    sent_far(enc_all, 2)
    sent_near(tok_all, 0)
    sent_near(cot_all, 1)
    sent_near(enc_all, 2)


def attend_kernel(
    n_mp, q, da, keys, values, wk_hbm, wv_hbm, wo_hbm, enc_terms, branches,
    dk, dv, att, att16, wk, wv, wo, w_sem,
):
    loads = [
        pltpu.make_async_copy(a, b, w_sem.at[i])
        for i, (a, b) in enumerate([(wk_hbm, wk), (wv_hbm, wv), (wo_hbm, wo)])
    ]
    for load in loads:
        load.start()
    seq_len, head_cols = q.shape
    readings, _, width = dk.shape[0], dk.shape[1], wk.shape[0]
    share = NLEN // n_mp
    feat = wo.shape[1] // n_mp
    factor = HD ** (-0.5)

    def one_block(b, _):
        rows = pl.ds(pl.multiple_of(b * BLOCK, BLOCK), BLOCK)
        mem = pl.ds(b * NEIGH, NEIGH)
        for h in range(head_cols // HD):
            cols = slice(h * HD, (h + 1) * HD)
            q_h, da_h = q[rows, cols], da[rows, cols]
            k_h = keys[mem, :, cols].reshape(NEIGH * NLEN, HD)
            v_h = values[mem, :, cols].reshape(NEIGH * NLEN, HD)
            scores = lax.dot_general(q_h, k_h, NT, preferred_element_type=F32) * factor
            lifted = jnp.exp(scores - jnp.max(scores, axis=-1, keepdims=True))
            prob = lifted / jnp.sum(lifted, axis=-1, keepdims=True)
            weights = prob.astype(BF16)
            att[rows, cols] = jnp.dot(weights, v_h, preferred_element_type=F32)
            d_prob = lax.dot_general(da_h, v_h, NT, preferred_element_type=F32)
            inner = jnp.sum(prob * d_prob, axis=-1, keepdims=True)
            d_scores = (prob * (d_prob - inner) * factor).astype(BF16)
            dv_h = lax.dot_general(weights, da_h, TN, preferred_element_type=F32).astype(BF16)
            dk_h = lax.dot_general(d_scores, q_h, TN, preferred_element_type=F32).astype(BF16)
            dv[mem, :, cols] = dv_h.reshape(NEIGH, NLEN, HD)
            dk[mem, :, cols] = dk_h.reshape(NEIGH, NLEN, HD)
        return 0

    lax.fori_loop(0, seq_len // BLOCK, one_block, 0)
    low = lax.broadcasted_iota(jnp.int32, (seq_len, head_cols), 0) >= LEAD
    att16[...] = jnp.where(low, pltpu.roll(att[...], LEAD, 0), 0.0).astype(BF16)
    loads[0].wait()
    loads[1].wait()

    def enc_chunk(k, _):
        toks = pl.ds(pl.multiple_of(k * share, share), share)
        acc = lax.dot_general(
            dk[:, toks, :].reshape(readings * share, head_cols), wk[...], NT,
            preferred_element_type=F32,
        )
        acc += lax.dot_general(
            dv[:, toks, :].reshape(readings * share, head_cols), wv[...], NT,
            preferred_element_type=F32,
        )
        enc_terms[k] = acc.astype(BF16).reshape(readings, share, width)
        return 0

    lax.fori_loop(0, n_mp, enc_chunk, 0)
    loads[2].wait()

    def branch_chunk(k, _):
        cols = pl.ds(pl.multiple_of(k * feat, feat), feat)
        branches[k] = jnp.dot(att16[...], wo[:, cols], preferred_element_type=F32).astype(BF16)
        return 0

    lax.fori_loop(0, n_mp, branch_chunk, 0)


def scatter_kernel(
    n_dp, n_mp,
    enc_terms, branches, tok, gain_post, enc, gain_enc, inverse, asker,
    mixed_out, ffn_out, denc_out,
    e_near, e_pair, e_far, b_near, b_pair, b_far, d_norm, back_out, back_in, sq_mine, sq_all,
    near_send, near_recv, far_send, far_recv, row_send, row_recv, sq_send, sq_recv,
):
    d, m, n_x, x, c, partner = place(n_dp, n_mp)
    own_rows = enc.shape[0]
    seq_len, feat = tok.shape
    greet(n_dp, n_mp, d, m)

    def near(buf, land, t, i):
        return pltpu.make_async_remote_copy(
            src_ref=buf.at[i * 2 + 1 - c], dst_ref=land.at[i],
            send_sem=near_send.at[t, i], recv_sem=near_recv.at[t, i],
            device_id=(d, partner), device_id_type=MESH,
        )

    def far(buf, land, t, o):
        to = (x + o) % n_x
        return pltpu.make_async_remote_copy(
            src_ref=buf.at[to], dst_ref=land.at[o],
            send_sem=far_send.at[t, o], recv_sem=far_recv.at[t, o],
            device_id=(d, to * 2 + c), device_id_type=MESH,
        )

    def row_copy(s, src, dst):
        return pltpu.make_async_remote_copy(
            src_ref=back_out.at[src], dst_ref=back_in.at[dst],
            send_sem=row_send.at[s], recv_sem=row_recv.at[s],
            device_id=((d + s) % n_dp, m), device_id_type=MESH,
        )

    def sq_copy(s):
        return pltpu.make_async_remote_copy(
            src_ref=sq_mine, dst_ref=sq_all.at[s], send_sem=sq_send.at[s], recv_sem=sq_recv.at[s],
            device_id=(d, (m + s) % n_mp), device_id_type=MESH,
        )

    sets = ((enc_terms, e_near, e_pair, e_far), (branches, b_near, b_pair, b_far))
    for t, (buf, land, _, _) in enumerate(sets):
        for i in range(n_x):
            near(buf, land, t, i).start()
    for t, (buf, land, pair, beyond) in enumerate(sets):
        for i in range(n_x):
            near(buf, land, t, i).wait_recv()
        for i in range(n_x):
            pair[i] = (buf[i * 2 + c].astype(F32) + land[i].astype(F32)).astype(BF16)
        for o in range(1, n_x):
            far(pair, beyond, t, o).start()
    total = e_pair[x].astype(F32)
    for o in range(1, n_x):
        far(e_pair, e_far, 0, o).wait_recv()
        total = total + e_far[o].astype(F32)
    d_norm[...] = total.astype(BF16)
    back_in[d] = d_norm[inverse[d]]
    for s in range(1, n_dp):
        holder = (d + s) % n_dp
        back_out[holder] = d_norm[inverse[holder]]
        row_copy(s, holder, d).start()
    added = b_pair[x].astype(F32)
    for o in range(1, n_x):
        far(b_pair, b_far, 1, o).wait_recv()
        added = added + b_far[o].astype(F32)
    mixed = (tok[...].astype(F32) + added).astype(BF16)
    mixed_out[...] = mixed
    wide = mixed.astype(F32)
    squares = jnp.broadcast_to(jnp.sum(wide * wide, axis=-1, keepdims=True), (seq_len, 128))
    sq_mine[...] = jnp.transpose(squares)[:8]
    for s in range(1, n_mp):
        sq_copy(s).start()
    for s in range(1, n_dp):
        source = (d + n_dp - s) % n_dp
        row_copy(s, source, source).wait_recv()
    for row in range(own_rows):
        wide = enc[row].astype(F32)
        scale = rms_scale(wide)
        hat = wide * scale
        up = gain_enc[...] * back_in[asker[row]].astype(F32)
        inner = jnp.mean(up * hat, axis=-1, keepdims=True)
        denc_out[row] = (scale * (up - hat * inner)).astype(BF16)
    squares = sq_mine[...]
    for s in range(1, n_mp):
        sq_copy(s).wait_recv()
        squares = squares + sq_all[s]
    squares = jnp.transpose(jnp.broadcast_to(squares[:1], (128, seq_len)))[:, :1]
    scale = lax.rsqrt(squares / (feat * n_mp) + EPS)
    ffn_out[...] = (mixed_out[...].astype(F32) * scale * gain_post[m]).astype(BF16)
    for t, (buf, land, pair, beyond) in enumerate(sets):
        for i in range(n_x):
            near(buf, land, t, i).wait_send()
        for o in range(1, n_x):
            far(pair, beyond, t, o).wait_send()
    for s in range(1, n_dp):
        row_copy(s, (d + s) % n_dp, d).wait_send()
    for s in range(1, n_mp):
        sq_copy(s).wait_send()


def shards(
    tokens, cotangent, gain_dec, w_query, w_out, encodings, gain_enc, w_key, w_value, gain_post,
    neighbour_ids,
):
    n_dp, n_mp = lax.axis_size("dp"), lax.axis_size("mp")
    n_x = n_mp // 2
    seq_len, feat = tokens.shape
    head_cols = w_query.shape[1]
    own_rows, share, width = encodings.shape
    readings = neighbour_ids.shape[0] * neighbour_ids.shape[1]
    chosen = neighbour_ids.reshape(readings)
    owner = chosen // own_rows
    ids = jnp.broadcast_to(chosen[:, None], (readings, 128))
    vmem = pl.BlockSpec(memory_space=pltpu.VMEM)
    smem = pl.BlockSpec(memory_space=pltpu.SMEM)
    anywhere = pl.BlockSpec(memory_space=pl.ANY)
    dma = pltpu.SemaphoreType.DMA
    shape = jax.ShapeDtypeStruct
    limit = 58 * 1024 * 1024
    gain_enc = gain_enc.reshape(1, width)
    queries, d_att, keys, values, idtab = pl.pallas_call(
        functools.partial(gather_kernel, n_dp, n_mp),
        out_shape=(
            shape((seq_len, head_cols), BF16),
            shape((seq_len, head_cols), BF16),
            shape((readings, NLEN, head_cols), BF16),
            shape((readings, NLEN, head_cols), BF16),
            shape((n_dp, readings, 128), jnp.int32),
        ),
        in_specs=[vmem, vmem, vmem, anywhere, anywhere, vmem, vmem, anywhere, anywhere, vmem, smem],
        out_specs=(vmem,) * 5,
        scratch_shapes=[
            pltpu.VMEM((n_mp, seq_len, feat), BF16),
            pltpu.VMEM((n_mp, seq_len, feat), BF16),
            pltpu.VMEM((n_mp, readings, share, width), BF16),
            pltpu.VMEM((n_mp, seq_len, feat), BF16),
            pltpu.VMEM((n_mp, feat, head_cols), BF16),
            pltpu.VMEM(w_out.shape, BF16),
            pltpu.VMEM(w_key.shape, BF16),
            pltpu.VMEM(w_value.shape, BF16),
            pltpu.VMEM((own_rows, share, width), F32),
            pltpu.VMEM((n_dp, share, width), BF16),
            pltpu.VMEM((n_dp, share, width), BF16),
            dma((4,)),
            dma((3, 2 * n_x)),
            dma((3, 2 * n_x)),
            dma((n_dp,)),
            dma((n_dp,)),
            dma((n_dp,)),
            dma((n_dp,)),
        ],
        compiler_params=pltpu.CompilerParams(
            collective_id=0, has_side_effects=True, vmem_limit_bytes=limit
        ),
        name="gather_project",
    )(
        tokens, cotangent, gain_dec.reshape(n_mp, 1, feat), w_query.reshape(n_mp, feat, head_cols),
        w_out, encodings, gain_enc, w_key, w_value, ids, owner,
    )
    enc_terms, branches = pl.pallas_call(
        functools.partial(attend_kernel, n_mp),
        out_shape=(
            shape((n_mp, readings, share, width), BF16),
            shape((n_mp, seq_len, feat), BF16),
        ),
        in_specs=[vmem] * 4 + [anywhere] * 3,
        out_specs=(vmem, vmem),
        scratch_shapes=[
            pltpu.VMEM((readings, NLEN, head_cols), BF16),
            pltpu.VMEM((readings, NLEN, head_cols), BF16),
            pltpu.VMEM((seq_len, head_cols), F32),
            pltpu.VMEM((seq_len, head_cols), BF16),
            pltpu.VMEM(w_key.shape, BF16),
            pltpu.VMEM(w_value.shape, BF16),
            pltpu.VMEM(w_out.shape, BF16),
            dma((3,)),
        ],
        compiler_params=pltpu.CompilerParams(vmem_limit_bytes=limit),
        name="attend",
    )(queries, d_att, keys, values, w_key, w_value, w_out)
    places = jnp.arange(n_dp, dtype=jnp.int32)
    order = jnp.arange(readings, dtype=jnp.int32)
    inverse = jnp.sum(
        jnp.where(owner[None, :] == places[:, None], order[None, :], 0), axis=1, dtype=jnp.int32
    )
    held = lax.axis_index("dp") * own_rows + jnp.arange(own_rows, dtype=jnp.int32)
    asks = jnp.any(idtab[:, :, 0][None] == held[:, None, None], axis=2)
    asker = jnp.sum(jnp.where(asks, places[None, :], 0), axis=1, dtype=jnp.int32)
    return pl.pallas_call(
        functools.partial(scatter_kernel, n_dp, n_mp),
        out_shape=(
            shape((seq_len, feat), BF16),
            shape((seq_len, feat), BF16),
            shape((own_rows, share, width), BF16),
        ),
        in_specs=[vmem] * 6 + [smem] * 2,
        out_specs=(vmem,) * 3,
        scratch_shapes=[
            pltpu.VMEM((n_x, readings, share, width), BF16),
            pltpu.VMEM((n_x, readings, share, width), BF16),
            pltpu.VMEM((n_x, readings, share, width), BF16),
            pltpu.VMEM((n_x, seq_len, feat), BF16),
            pltpu.VMEM((n_x, seq_len, feat), BF16),
            pltpu.VMEM((n_x, seq_len, feat), BF16),
            pltpu.VMEM((readings, share, width), BF16),
            pltpu.VMEM((n_dp, share, width), BF16),
            pltpu.VMEM((n_dp, share, width), BF16),
            pltpu.VMEM((8, seq_len), F32),
            pltpu.VMEM((n_mp, 8, seq_len), F32),
            dma((2, n_x)),
            dma((2, n_x)),
            dma((2, n_x)),
            dma((2, n_x)),
            dma((n_dp,)),
            dma((n_dp,)),
            dma((n_mp,)),
            dma((n_mp,)),
        ],
        compiler_params=pltpu.CompilerParams(
            collective_id=1, has_side_effects=True, vmem_limit_bytes=limit
        ),
        name="reduce_return",
    )(
        enc_terms, branches, tokens, gain_post.reshape(n_mp, 1, feat), encodings, gain_enc,
        inverse, asker,
    )


def solution(mesh):
    in_specs = (
        P("dp", "mp"),
        P("dp", "mp"),
        P(),
        P(None, "mp"),
        P("mp", None),
        P("dp", "mp", None),
        P(),
        P(None, "mp"),
        P(None, "mp"),
        P(),
        P("dp", None),
    )
    out_specs = (P("dp", "mp"), P("dp", "mp"), P("dp", "mp", None))
    return jax.shard_map(shards, mesh=mesh, in_specs=in_specs, out_specs=out_specs, check_vma=False)
```

time: 247 us -> 120 us (0.49)
  Pallas kernels: 0 us -> 110 us
  waiting for transfers between devices: 93.3 us -> 0 us
  matrix products: 72.9 us -> 0 us
  local copies, waits for them, and re-layouts: 27.9 us -> 7.56 us
  blocking collectives: 14.4 us -> 0 us
  between operations: 14 us -> 0.71 us
  starting transfers between devices: 13.2 us -> 0 us
  other arithmetic: 10.3 us -> 1.48 us
    pallas_call x0 -> x3, Pallas kernels: none -> 110 us  [the longest x1 49.8 us: shards(): pl.pallas_call(functools.partial(gather_kernel, n_dp, n_mp), out_shape=(s...]
    dot_general x14 -> x0, matrix products: 72.9 us -> none  [the longest x1 16.5 us: shards(): jnp.einsum('chqk,cqhd->ckhd', d_scores, shifted, preferred_element_type=j...]
    psum x1 -> x0, waiting for transfers between devices: 45.8 us -> none  [shards(): summed = lax.psum(branch.astype(jnp.bfloat16), 'mp').astype(jnp.float32)]
    all_gather x3 -> x0, waiting for transfers between devices: 25.2 us -> none  [the longest x1 15 us: shards(): lax.all_gather(picked, 'mp', axis=1, tiled=True)]
    reduce_scatter x1 -> x0, waiting for transfers between devices: 15.7 us -> none  [shards(): lax.psum_scatter(jnp.einsum('atj,ej->tae', both_grads, w_both, preferred_...]
    all_to_all x1 -> x0, blocking collectives: 14.4 us -> none  [shards(): lax.all_to_all(outgoing, 'dp', split_axis=0, concat_axis=0, tiled=True)]
    convert_element_type x5 -> x0, local copies, waits for them, and re-layouts: 13 us -> none  [the longest x1 4.33 us: shards(): key_grad = jnp.einsum('chqk,cqhd->ckhd', d_scores, shifted, preferred_ele...]
    all_to_all x2 -> x0, starting transfers between devices: 12.8 us -> none  [the longest x1 7.28 us: shards(): lax.all_to_all(wanted.reshape(dp_count, per_holder), 'dp', split_axis=0,...]
  transfers between devices with their start and end apart: 7 -> 0, of which waited for: 5 -> 0; matrix products, arithmetic and copies ran while one was open for 17% -> 0% of each run, Pallas kernels for 0% -> 0%
where the time goes in v1:
time: 120 us
  Pallas kernels  110 us (92%)
  local copies, waits for them, and re-layouts  7.56 us (6%)
  other arithmetic  1.48 us (1%)
    pallas_call x1, Pallas kernels, shards(): pl.pallas_call(functools.partial(gather_kernel, n_dp, n_mp), out_shape=(s...  49.8 us
    pallas_call x1, Pallas kernels, shards(): pl.pallas_call(functools.partial(scatter_kernel, n_dp, n_mp), out_shape=(...  34.8 us
    pallas_call x1, Pallas kernels, shards(): pl.pallas_call(functools.partial(attend_kernel, n_mp), out_shape=(shape((...  25.5 us
    unnamed x10, local copies, waits for them, and re-layouts  5.34 us

profile of v1, /device:TPU:0, one launch (start us, length us, event | category | flops | bytes accessed | tf_op | source)
XLA Modules:
  0.0 119.8 jit_solution(13938235460919870365)
XLA Ops:
  0.6 0.8 copy.16
  1.4 0.1 broadcast_in_dim.30
  1.5 0.5 and_select_fusion.owner
  2.0 0.7 broadcast_in_dim.31.ids
  2.7 1.3 %reshape.55.gain_enc = f32[1,896]{1,0:T(1,128)} reshape(f32[896]{0:T(1024)} %param.17) | data formatting | bytes 7168 | tf_op jit(solution)/shard_map/reshape | solution.py:391
  3.9 49.8 %gather_project.1 = (bf16[256,1024]{1,0:T(8,128)(2,1)}, bf16[256,1024]{1,0:T(8,128)(2,1)}, bf16[8,128,1024]{2,1,0:T(8,128)(2,1)}, bf16[8,128,1024]{2,1,0:T(8,128)(2,1)}, s32[8,8,128]{2,1,0:T(8,128)}) custom-call(bf16[256,1024]{1,0:T(8,128)(2,1)} %tok.3, bf16[256,1024]{1,0:T(8,128)(2,1)} %cot.1, f32[4,1,1024]{2,1,0:T(1,128)} %bitcast.5, ...), custom_call_target="tpu_custom_call" | custom-call | tf_op jit(solution)/shard_map/gather_project/pallas_call | solution.py:392
  53.7 0.0 copy-start.1
  53.7 0.0 copy-start.2
  53.7 25.5 %attend.1 = (bf16[4,8,32,896]{3,2,1,0:T(8,128)(2,1)}, bf16[4,256,1024]{2,1,0:T(8,128)(2,1)}) custom-call(bf16[256,1024]{1,0:T(8,128)(2,1)} %get-tuple-element.10.q, bf16[256,1024]{1,0:T(8,128)(2,1)} %get-tuple-element.11.da, bf16[8,128,1024]{2,1,0:T(8,128)(2,1)} %get-tuple-element.12.keys, bf16[8,128,1024]{2,1,0:T(8,128)(2,1)} %get-tuple-element.13.values, ...), custom_call_target="tpu_custom_call" | custom-call | tf_op jit(solution)/shard_map/attend/pallas_call | solution.py:431
  79.3 0.0 copy-done.1
  79.3 0.2 slice_reduce_fusion
  79.5 0.3 compare_reduce_fusion
  79.8 0.0 copy-done.2
  79.8 0.7 select_reduce_fusion
  80.5 34.8 %reduce_return.1 = (bf16[256,1024]{1,0:T(8,128)(2,1)}, bf16[256,1024]{1,0:T(8,128)(2,1)}, bf16[8,32,896]{2,1,0:T(8,128)(2,1)}) custom-call(bf16[4,8,32,896]{3,2,1,0:T(8,128)(2,1)} %get-tuple-element.14.enc_terms, bf16[4,256,1024]{2,1,0:T(8,128)(2,1)} %get-tuple-element.15.branches, bf16[256,1024]{1,0:T(8,128)(2,1)} %tok.3, f32[4,1,1024]{2,1,0:T(1,128)} %bitcast.4, ...), custom_call_target="tpu_custom_call" | custom-call | tf_op jit(solution)/shard_map/reduce_return/pallas_call | solution.py:460
  115.3 0.0 copy-start
  115.3 1.9 %copy.20 = bf16[256,1024]{1,0:T(8,128)(2,1)} copy(bf16[256,1024]{1,0:T(8,128)(2,1)} %get-tuple-element.22) | data formatting | bytes 1048576
  117.2 1.9 %copy.21 = bf16[256,1024]{1,0:T(8,128)(2,1)} copy(bf16[256,1024]{1,0:T(8,128)(2,1)} %get-tuple-element.23) | data formatting | bytes 1048576
  119.1 0.0 copy-done
  119.1 0.8 copy.22
  (1 shorter events, 0.0 us)
Async XLA Ops:
  53.7 25.6 %copy-start.1 = (s32[8,8,128]{2,1,0:T(8,128)S(1)}, s32[8,8,128]{2,1,0:T(8,128)}, u32[]{:S(2)}) copy-start(s32[8,8,128]{2,1,0:T(8,128)} %get-tuple-element.16) | copy-start | bytes 98308
  53.7 26.1 %copy-start.2 = (s32[8]{0:T(128)S(1)}, s32[8]{0:T(128)}, u32[]{:S(2)}) copy-start(s32[8]{0:T(128)} %and_select_fusion.owner) | copy-start | bytes 100
  115.3 3.8 %copy-start = (bf16[8,32,896]{2,1,0:T(8,128)(2,1)S(1)}, bf16[8,32,896]{2,1,0:T(8,128)(2,1)}, u32[]{:S(2)}) copy-start(bf16[8,32,896]{2,1,0:T(8,128)(2,1)} %get-tuple-element.24) | copy-start | bytes 1376260

commit v2 on v0

v2 whole, which is shorter than its diff:
```python
import functools

import jax
import jax.numpy as jnp
from jax import lax
from jax.experimental import pallas as pl
from jax.experimental.pallas import tpu as pltpu
from jax.sharding import PartitionSpec as P

HD = 128
BLOCK = 64
NLEN = 128
NEIGH = 2
LEAD = BLOCK - 1
EPS = 1e-06
MESH = pl.DeviceIdType.MESH
BF16 = jnp.bfloat16
F32 = jnp.float32
NT = (((1,), (1,)), ((), ()))
TN = (((0,), (0,)), ((), ()))


def rms_scale(values):
    return lax.rsqrt(jnp.mean(values * values, axis=-1, keepdims=True) + EPS)


def place(n_dp, n_mp):
    d, m = lax.axis_index("dp"), lax.axis_index("mp")
    n_x = n_mp // 2
    x, c = m // 2, m % 2
    return d, m, n_x, x, c, x * 2 + (1 - c)


def greet(n_dp, n_mp, d, m):
    barrier = pltpu.get_barrier_semaphore()
    for s in range(1, n_dp):
        pl.semaphore_signal(barrier, inc=1, device_id=((d + s) % n_dp, m), device_id_type=MESH)
    for s in range(1, n_mp):
        pl.semaphore_signal(barrier, inc=1, device_id=(d, (m + s) % n_mp), device_id_type=MESH)
    pl.semaphore_wait(barrier, n_dp + n_mp - 2)


def layer_kernel(
    n_dp, n_mp,
    tok, cot, gain_dec, wq_hbm, wo_hbm, enc, gain_enc, wk_hbm, wv_hbm, chosen,
    mixed_out, squares_out, rows_out,
    tok_all, cot_a, cot_b, enc_all, normed, wq, wo, wk, wv, enc_norm, sending, arrived, ids, idtab,
    q, da, keys, values, prob_all, att, att16, dk, dv,
    enc_terms, branches, e_near, e_pair, e_far, b_near, b_pair, b_far,
    d_norm, back_out, back_in, sq_mine, sq_all,
    w_sem, ag_send, ag_recv, id_send, id_recv, row_send, row_recv,
    near_send, near_recv, far_send, far_recv, back_send, back_recv, sq_send, sq_recv,
):
    d, m, n_x, x, c, partner = place(n_dp, n_mp)
    own_rows, share, width = enc.shape
    readings = ids.shape[0]
    seq_len, feat = tok.shape
    half = seq_len // 2
    head_cols = wq.shape[2]
    heads = head_cols // HD
    factor = HD ** (-0.5)
    loads = [
        pltpu.make_async_copy(a, b, w_sem.at[i])
        for i, (a, b) in enumerate([(wq_hbm, wq), (wo_hbm, wo), (wk_hbm, wk), (wv_hbm, wv)])
    ]
    for i in (0, 2, 3, 1):
        loads[i].start()

    def hop(buf, t, kind, chunk, target):
        return pltpu.make_async_remote_copy(
            src_ref=buf.at[chunk], dst_ref=buf.at[chunk],
            send_sem=ag_send.at[t, kind], recv_sem=ag_recv.at[t, kind],
            device_id=(d, target), device_id_type=MESH,
        )

    def spread(buf, t):
        for o in range(1, n_x):
            hop(buf, t, o, m, ((x + o) % n_x) * 2 + c).start()
        hop(buf, t, 0, m, partner).start()

    def forward(buf, t):
        for o in range(1, n_x):
            chunk = ((x + n_x - o) % n_x) * 2 + c
            hop(buf, t, o, chunk, partner).wait_recv()
            hop(buf, t, n_x + o, chunk, partner).start()

    def finish(buf, t):
        hop(buf, t, 0, partner, partner).wait_recv()
        for o in range(1, n_x):
            hop(buf, t, n_x + o, ((x + n_x - o) % n_x) * 2 + 1 - c, partner).wait_recv()

    def sent_far(buf, t):
        for o in range(1, n_x):
            hop(buf, t, o, m, partner).wait_send()

    def sent_near(buf, t):
        hop(buf, t, 0, m, partner).wait_send()
        for o in range(1, n_x):
            hop(buf, t, n_x + o, m, partner).wait_send()

    def dp_copy(src, dst, send, recv, s):
        return pltpu.make_async_remote_copy(
            src_ref=src, dst_ref=dst, send_sem=send.at[s], recv_sem=recv.at[s],
            device_id=((d + s) % n_dp, m), device_id_type=MESH,
        )

    def id_copy(s, to):
        return dp_copy(ids, idtab.at[to], id_send, id_recv, s)

    def row_copy(s, src, dst):
        return dp_copy(sending.at[src], arrived.at[dst], row_send, row_recv, s)

    def back_copy(s, src, dst):
        return dp_copy(back_out.at[src], back_in.at[dst], back_send, back_recv, s)

    def near(buf, land, t, i):
        return pltpu.make_async_remote_copy(
            src_ref=buf.at[i * 2 + 1 - c], dst_ref=land.at[i],
            send_sem=near_send.at[t, i], recv_sem=near_recv.at[t, i],
            device_id=(d, partner), device_id_type=MESH,
        )

    def far(buf, land, t, o):
        to = (x + o) % n_x
        return pltpu.make_async_remote_copy(
            src_ref=buf.at[to], dst_ref=land.at[o],
            send_sem=far_send.at[t, o], recv_sem=far_recv.at[t, o],
            device_id=(d, to * 2 + c), device_id_type=MESH,
        )

    def sq_copy(s):
        return pltpu.make_async_remote_copy(
            src_ref=sq_mine, dst_ref=sq_all.at[s], send_sem=sq_send.at[s], recv_sem=sq_recv.at[s],
            device_id=(d, (m + s) % n_mp), device_id_type=MESH,
        )

    def pair_up(buf, land, pair, t):
        for i in range(n_x):
            near(buf, land, t, i).wait_recv()
        for o in range(1, n_x):
            to = (x + o) % n_x
            pair[to] = (buf[to * 2 + c].astype(F32) + land[to].astype(F32)).astype(BF16)

    tok_all[m] = tok[...]
    picks = [chosen[a // NEIGH, a % NEIGH] for a in range(readings)]
    spot = lax.broadcasted_iota(jnp.int32, (readings, 128), 0)
    listed = jnp.zeros((readings, 128), jnp.int32)
    for a in range(readings):
        listed = jnp.where(spot == a, picks[a], listed)
    ids[...] = listed
    greet(n_dp, n_mp, d, m)
    for s in range(1, n_dp):
        id_copy(s, d).start()
    spread(tok_all, 0)
    idtab[d] = listed
    cot_a[m] = cot[:half]
    cot_b[m] = cot[half:]
    wide = enc[...].astype(F32)
    enc_norm[...] = wide * rms_scale(wide) * gain_enc[...][None]

    def choose(reader):
        asked = idtab[reader]
        total = jnp.zeros((share, width), F32)
        for row in range(own_rows):
            hit = jnp.where(asked == d * own_rows + row, 1.0, 0.0).astype(F32)
            hit = jnp.max(hit, axis=0, keepdims=True)
            total = total + enc_norm[row] * jnp.concatenate([hit] * (width // 128), axis=1)
        return total.astype(BF16)

    for s in range(1, n_dp):
        reader = (d + s) % n_dp
        id_copy(n_dp - s, reader).wait_recv()
        sending[reader] = choose(reader)
        row_copy(s, reader, d).start()
    arrived[d] = choose(d)
    sent_far(tok_all, 0)
    spread(cot_a, 1)
    forward(tok_all, 0)
    table = idtab[...]
    owner_at = lax.broadcasted_iota(jnp.int32, table.shape, 0)
    askers = [
        jnp.max(jnp.where(table == d * own_rows + row, owner_at, 0)) for row in range(own_rows)
    ]
    for s in range(1, n_dp):
        holder = (d + n_dp - s) % n_dp
        row_copy(s, holder, holder).wait_recv()
    for a in range(readings):
        enc_all[m, a] = arrived[picks[a] // own_rows]
    spread(enc_all, 3)
    finish(tok_all, 0)
    squares = jnp.zeros((seq_len, 1), F32)
    for k in range(n_mp):
        part = tok_all[k].astype(F32)
        squares = squares + jnp.sum(part * part, axis=-1, keepdims=True)
    scale = lax.rsqrt(squares / (feat * n_mp) + EPS)
    for k in range(n_mp):
        normed[k] = (tok_all[k].astype(F32) * scale * gain_dec[k]).astype(BF16)
    loads[0].wait()
    keep = lax.broadcasted_iota(jnp.int32, (seq_len, 256), 0) < seq_len - LEAD

    def shift_up(part):
        return jnp.where(keep, pltpu.roll(part, seq_len - LEAD, 0), 0.0).astype(BF16)

    def query_tile(n, _):
        cols = pl.ds(pl.multiple_of(n * 256, 256), 256)
        acc = jnp.zeros((seq_len, 256), F32)
        for k in range(n_mp):
            acc += jnp.dot(normed[k], wq[k, :, cols], preferred_element_type=F32)
        q[:, cols] = shift_up(acc)
        return 0

    lax.fori_loop(0, head_cols // 256, query_tile, 0)
    forward(cot_a, 1)
    sent_far(enc_all, 3)
    spread(cot_b, 2)
    forward(enc_all, 3)
    finish(enc_all, 3)
    loads[2].wait()
    loads[3].wait()

    def memory_tile(n, _):
        cols = pl.ds(pl.multiple_of(n * 256, 256), 256)
        for k in range(n_mp):
            rows = enc_all[k].reshape(readings * share, width)
            for weight, out in ((wk, keys), (wv, values)):
                part = jnp.dot(rows, weight[:, cols], preferred_element_type=F32).astype(BF16)
                out[:, k * share : (k + 1) * share, cols] = part.reshape(readings, share, 256)
        return 0

    lax.fori_loop(0, head_cols // 256, memory_tile, 0)

    def memory_of(buf, b, h):
        part = buf[pl.ds(b * NEIGH, NEIGH), :, h * HD : (h + 1) * HD]
        return part.reshape(NEIGH * NLEN, HD)

    def attend(b, _):
        rows = pl.ds(pl.multiple_of(b * BLOCK, BLOCK), BLOCK)
        for h0 in range(0, heads, 4):
            group = range(h0, h0 + 4)
            scores = [
                lax.dot_general(
                    q[rows, h * HD : (h + 1) * HD], memory_of(keys, b, h), NT,
                    preferred_element_type=F32,
                ) * factor
                for h in group
            ]
            lifted = [jnp.exp(v - jnp.max(v, axis=-1, keepdims=True)) for v in scores]
            prob = [v / jnp.sum(v, axis=-1, keepdims=True) for v in lifted]
            for h, v in zip(group, prob):
                prob_all[b, h] = v
            for h, v in zip(group, prob):
                att[rows, h * HD : (h + 1) * HD] = jnp.dot(
                    v.astype(BF16), memory_of(values, b, h), preferred_element_type=F32
                )
        return 0

    lax.fori_loop(0, seq_len // BLOCK, attend, 0)
    low = lax.broadcasted_iota(jnp.int32, (seq_len, head_cols), 0) >= LEAD
    att16[...] = jnp.where(low, pltpu.roll(att[...], LEAD, 0), 0.0).astype(BF16)
    loads[1].wait()

    def branch_chunk(k, _):
        cols = pl.ds(pl.multiple_of(k * feat, feat), feat)
        branches[k] = jnp.dot(att16[...], wo[:, cols], preferred_element_type=F32).astype(BF16)
        return 0

    lax.fori_loop(0, n_mp, branch_chunk, 0)
    for i in range(n_x):
        near(branches, b_near, 1, i).start()
    forward(cot_b, 2)
    pair_up(branches, b_near, b_pair, 1)
    for o in range(1, n_x):
        far(b_pair, b_far, 1, o).start()
    finish(cot_a, 1)
    finish(cot_b, 2)

    def grad_tile(n, _):
        cols = pl.ds(pl.multiple_of(n * 256, 256), 256)
        acc = jnp.zeros((seq_len, 256), F32)
        for k in range(n_mp):
            acc += lax.dot_general(
                jnp.concatenate([cot_a[k], cot_b[k]], axis=0),
                wo[cols, k * feat : (k + 1) * feat], NT, preferred_element_type=F32,
            )
        da[:, cols] = shift_up(acc)
        return 0

    lax.fori_loop(0, head_cols // 256, grad_tile, 0)

    def attend_back(b, _):
        rows = pl.ds(pl.multiple_of(b * BLOCK, BLOCK), BLOCK)
        mem = pl.ds(b * NEIGH, NEIGH)
        for h0 in range(0, heads, 4):
            group = range(h0, h0 + 4)
            d_prob = [
                lax.dot_general(
                    da[rows, h * HD : (h + 1) * HD], memory_of(values, b, h), NT,
                    preferred_element_type=F32,
                )
                for h in group
            ]
            for h in group:
                cols = slice(h * HD, (h + 1) * HD)
                dv_h = lax.dot_general(
                    prob_all[b, h].astype(BF16), da[rows, cols], TN, preferred_element_type=F32
                )
                dv[mem, :, cols] = dv_h.astype(BF16).reshape(NEIGH, NLEN, HD)
            d_scores = []
            for h, v in zip(group, d_prob):
                prob = prob_all[b, h]
                inner = jnp.sum(prob * v, axis=-1, keepdims=True)
                d_scores.append((prob * (v - inner) * factor).astype(BF16))
            for h, v in zip(group, d_scores):
                cols = slice(h * HD, (h + 1) * HD)
                dk_h = lax.dot_general(v, q[rows, cols], TN, preferred_element_type=F32)
                dk[mem, :, cols] = dk_h.astype(BF16).reshape(NEIGH, NLEN, HD)
        return 0

    lax.fori_loop(0, seq_len // BLOCK, attend_back, 0)

    def enc_chunk(k):
        toks = pl.ds(pl.multiple_of(k * share, share), share)
        acc = lax.dot_general(
            dk[:, toks, :].reshape(readings * share, head_cols), wk[...], NT,
            preferred_element_type=F32,
        )
        acc += lax.dot_general(
            dv[:, toks, :].reshape(readings * share, head_cols), wv[...], NT,
            preferred_element_type=F32,
        )
        enc_terms[k] = acc.astype(BF16).reshape(readings, share, width)

    def partner_chunk(i, _):
        enc_chunk(i * 2 + 1 - c)
        near(enc_terms, e_near, 0, i).start()
        return 0

    def own_chunk(i, _):
        enc_chunk(i * 2 + c)
        return 0

    lax.fori_loop(0, n_x, partner_chunk, 0)
    lax.fori_loop(0, n_x, own_chunk, 0)
    pair_up(enc_terms, e_near, e_pair, 0)
    for o in range(1, n_x):
        far(e_pair, e_far, 0, o).start()
    added = branches[m].astype(F32) + b_near[x].astype(F32)
    for o in range(1, n_x):
        far(b_pair, b_far, 1, o).wait_recv()
        added = added + b_far[o].astype(F32)
    mixed = (tok[...].astype(F32) + added).astype(BF16)
    mixed_out[...] = mixed
    wide = mixed.astype(F32)
    squares = jnp.broadcast_to(jnp.sum(wide * wide, axis=-1, keepdims=True), (seq_len, 128))
    sq_mine[...] = jnp.transpose(squares)[:8]
    for s in range(1, n_mp):
        sq_copy(s).start()
    total = enc_terms[m].astype(F32) + e_near[x].astype(F32)
    for o in range(1, n_x):
        far(e_pair, e_far, 0, o).wait_recv()
        total = total + e_far[o].astype(F32)
    d_norm[...] = total.astype(BF16)

    def reading_of(holder):
        found = jnp.int32(0)
        for a in range(readings):
            found = jnp.where(picks[a] // own_rows == holder, a, found)
        return found

    for s in range(1, n_dp):
        holder = (d + s) % n_dp
        back_out[holder] = d_norm[reading_of(holder)]
        back_copy(s, holder, d).start()
    back_in[d] = d_norm[reading_of(d)]
    squares = sq_mine[...]
    for s in range(1, n_mp):
        sq_copy(s).wait_recv()
        squares = squares + sq_all[s]
    squares_out[...] = squares
    for s in range(1, n_dp):
        source = (d + n_dp - s) % n_dp
        back_copy(s, source, source).wait_recv()
    for row in range(own_rows):
        rows_out[row] = back_in[askers[row]]
    sent_far(cot_a, 1)
    sent_far(cot_b, 2)
    for t, buf in enumerate((tok_all, cot_a, cot_b, enc_all)):
        sent_near(buf, t)
    for t, (buf, land, pair, beyond) in enumerate(
        ((enc_terms, e_near, e_pair, e_far), (branches, b_near, b_pair, b_far))
    ):
        for i in range(n_x):
            near(buf, land, t, i).wait_send()
        for o in range(1, n_x):
            far(pair, beyond, t, o).wait_send()
    for s in range(1, n_dp):
        to = (d + s) % n_dp
        id_copy(s, d).wait_send()
        row_copy(s, to, d).wait_send()
        back_copy(s, to, d).wait_send()
    for s in range(1, n_mp):
        sq_copy(s).wait_send()


def finish_kernel(n_mp, mixed, squares, rows, enc, gain_enc, gain_post, mixed_out, ffn_out, denc_out):
    seq_len, feat = mixed.shape
    mixed_out[...] = mixed[...]
    scale = jnp.transpose(jnp.broadcast_to(squares[:1], (128, seq_len)))[:, :1]
    scale = lax.rsqrt(scale / (feat * n_mp) + EPS)
    gain = gain_post[lax.axis_index("mp")]
    ffn_out[...] = (mixed[...].astype(F32) * scale * gain).astype(BF16)
    for row in range(enc.shape[0]):
        wide = enc[row].astype(F32)
        scale = rms_scale(wide)
        hat = wide * scale
        up = gain_enc[...] * rows[row].astype(F32)
        inner = jnp.mean(up * hat, axis=-1, keepdims=True)
        denc_out[row] = (scale * (up - hat * inner)).astype(BF16)


def shards(
    tokens, cotangent, gain_dec, w_query, w_out, encodings, gain_enc, w_key, w_value, gain_post,
    neighbour_ids,
):
    n_dp, n_mp = lax.axis_size("dp"), lax.axis_size("mp")
    n_x = n_mp // 2
    seq_len, feat = tokens.shape
    head_cols = w_query.shape[1]
    own_rows, share, width = encodings.shape
    blocks = neighbour_ids.shape[0]
    readings = blocks * neighbour_ids.shape[1]
    block = pl.BlockSpec(memory_space=pltpu.VMEM)
    smem = pl.BlockSpec(memory_space=pltpu.SMEM)
    anywhere = pl.BlockSpec(memory_space=pl.ANY)
    dma = pltpu.SemaphoreType.DMA
    shape = jax.ShapeDtypeStruct
    vmem = pltpu.VMEM
    gain_enc = gain_enc.reshape(1, width)
    tokens_all = vmem((n_mp, seq_len, feat), BF16)
    half_all = vmem((n_mp, seq_len // 2, feat), BF16)
    rows_all = vmem((n_mp, readings, share, width), BF16)
    slots = vmem((n_dp, share, width), BF16)
    local = vmem((seq_len, head_cols), BF16)
    memory = vmem((readings, NLEN, head_cols), BF16)
    rows_x = vmem((n_x, readings, share, width), BF16)
    tokens_x = vmem((n_x, seq_len, feat), BF16)
    mixed, squares, rows = pl.pallas_call(
        functools.partial(layer_kernel, n_dp, n_mp),
        out_shape=(
            shape((seq_len, feat), BF16),
            shape((8, seq_len), F32),
            shape((own_rows, share, width), BF16),
        ),
        in_specs=[block] * 3 + [anywhere] * 2 + [block] * 2 + [anywhere] * 2 + [smem],
        out_specs=(block,) * 3,
        scratch_shapes=[
            tokens_all, half_all, half_all, rows_all, tokens_all,
            vmem((n_mp, feat, head_cols), BF16),
            vmem(w_out.shape, BF16),
            vmem(w_key.shape, BF16),
            vmem(w_value.shape, BF16),
            vmem((own_rows, share, width), F32),
            slots, slots,
            vmem((readings, 128), jnp.int32),
            vmem((n_dp, readings, 128), jnp.int32),
            local, local, memory, memory,
            vmem((blocks, head_cols // HD, BLOCK, NEIGH * NLEN), F32),
            vmem((seq_len, head_cols), F32),
            local, memory, memory,
            rows_all, tokens_all,
            rows_x, rows_x, rows_x, tokens_x, tokens_x, tokens_x,
            vmem((readings, share, width), BF16),
            slots, slots,
            vmem((8, seq_len), F32),
            vmem((n_mp, 8, seq_len), F32),
            dma((4,)),
            dma((4, 2 * n_x)), dma((4, 2 * n_x)),
            dma((n_dp,)), dma((n_dp,)), dma((n_dp,)), dma((n_dp,)),
            dma((2, n_x)), dma((2, n_x)), dma((2, n_x)), dma((2, n_x)),
            dma((n_dp,)), dma((n_dp,)), dma((n_mp,)), dma((n_mp,)),
        ],
        compiler_params=pltpu.CompilerParams(
            collective_id=0, has_side_effects=True, vmem_limit_bytes=60 * 1024 * 1024
        ),
        name="layer",
    )(
        tokens, cotangent, gain_dec.reshape(n_mp, 1, feat), w_query.reshape(n_mp, feat, head_cols),
        w_out, encodings, gain_enc, w_key, w_value, neighbour_ids,
    )
    return pl.pallas_call(
        functools.partial(finish_kernel, n_mp),
        out_shape=(
            shape((seq_len, feat), BF16),
            shape((seq_len, feat), BF16),
            shape((own_rows, share, width), BF16),
        ),
        in_specs=[block] * 6,
        out_specs=(block,) * 3,
        name="finish",
    )(mixed, squares, rows, encodings, gain_enc, gain_post.reshape(n_mp, 1, feat))


def solution(mesh):
    in_specs = (
        P("dp", "mp"),
        P("dp", "mp"),
        P(),
        P(None, "mp"),
        P("mp", None),
        P("dp", "mp", None),
        P(),
        P(None, "mp"),
        P(None, "mp"),
        P(),
        P("dp", None),
    )
    out_specs = (P("dp", "mp"), P("dp", "mp"), P("dp", "mp", None))
    return jax.shard_map(shards, mesh=mesh, in_specs=in_specs, out_specs=out_specs, check_vma=False)
```

time: 247 us -> 91.8 us (0.37)
  waiting for transfers between devices: 93.3 us -> 0 us
  Pallas kernels: 0 us -> 88 us
  matrix products: 72.9 us -> 0 us
  local copies, waits for them, and re-layouts: 27.9 us -> 2.62 us
  blocking collectives: 14.4 us -> 0 us
  between operations: 14 us -> 0.64 us
  starting transfers between devices: 13.2 us -> 0 us
  other arithmetic: 10.3 us -> 0 us
    pallas_call x0 -> x2, Pallas kernels: none -> 88 us  [the longest x1 85 us: shards(): pl.pallas_call(functools.partial(layer_kernel, n_dp, n_mp), out_shape=(sh...]
    dot_general x14 -> x0, matrix products: 72.9 us -> none  [the longest x1 16.5 us: shards(): jnp.einsum('chqk,cqhd->ckhd', d_scores, shifted, preferred_element_type=j...]
    psum x1 -> x0, waiting for transfers between devices: 45.8 us -> none  [shards(): summed = lax.psum(branch.astype(jnp.bfloat16), 'mp').astype(jnp.float32)]
    all_gather x3 -> x0, waiting for transfers between devices: 25.2 us -> none  [the longest x1 15 us: shards(): lax.all_gather(picked, 'mp', axis=1, tiled=True)]
    reduce_scatter x1 -> x0, waiting for transfers between devices: 15.7 us -> none  [shards(): lax.psum_scatter(jnp.einsum('atj,ej->tae', both_grads, w_both, preferred_...]
    all_to_all x1 -> x0, blocking collectives: 14.4 us -> none  [shards(): lax.all_to_all(outgoing, 'dp', split_axis=0, concat_axis=0, tiled=True)]
    convert_element_type x5 -> x0, local copies, waits for them, and re-layouts: 13 us -> none  [the longest x1 4.33 us: shards(): key_grad = jnp.einsum('chqk,cqhd->ckhd', d_scores, shifted, preferred_ele...]
    all_to_all x2 -> x0, starting transfers between devices: 12.8 us -> none  [the longest x1 7.28 us: shards(): lax.all_to_all(wanted.reshape(dp_count, per_holder), 'dp', split_axis=0,...]
  transfers between devices with their start and end apart: 7 -> 0, of which waited for: 5 -> 0; matrix products, arithmetic and copies ran while one was open for 17% -> 0% of each run, Pallas kernels for 0% -> 0%
where the time goes in v2:
time: 91.8 us; the launch traced here: 91.2 us
  Pallas kernels  88 us (96%)
  local copies, waits for them, and re-layouts  2.62 us (3%)
    pallas_call x1, Pallas kernels, shards(): pl.pallas_call(functools.partial(layer_kernel, n_dp, n_mp), out_shape=(sh...  85 us
    pallas_call x1, Pallas kernels, shards(): pl.pallas_call(functools.partial(finish_kernel, n_mp), out_shape=(shape((...  2.93 us

profile of v2, /device:TPU:0, one launch (start us, length us, event | category | flops | bytes accessed | tf_op | source)
XLA Modules:
  0.0 91.2 jit_solution(7626338147975165517)
XLA Ops:
  0.6 1.3 %copy.14.chosen = s32[4,2]{1,0:T(4,128)} copy(s32[4,2]{0,1:T(2,128)} %param.21) | data formatting | bytes 64 | tf_op args[10]
  2.0 1.3 %reshape.20.gain_enc = f32[1,896]{1,0:T(1,128)} reshape(f32[896]{0:T(1024)} %param.17) | data formatting | bytes 7168 | tf_op jit(solution)/shard_map/reshape | solution.py:438
  3.3 85.0 %layer.1 = (bf16[256,1024]{1,0:T(8,128)(2,1)}, f32[8,256]{1,0:T(8,128)}, bf16[8,32,896]{2,1,0:T(8,128)(2,1)}) custom-call(bf16[256,1024]{1,0:T(8,128)(2,1)} %tok.1, bf16[256,1024]{1,0:T(8,128)(2,1)} %cot.1, f32[4,1,1024]{2,1,0:T(1,128)} %bitcast.4, bf16[4,1024,1024]{2,1,0:T(8,128)(2,1)} %bitcast.3, bf16[1024,4096]{1,0:T(8,128)(2,1)} %wo_hbm.1, ...), custom_call_target="tpu_custom_call" | custom-call | tf_op jit(solution)/shard_map/layer/pallas_call | solution.py:447
  88.3 2.9 %finish.1 = (bf16[256,1024]{1,0:T(8,128)(2,1)}, bf16[256,1024]{1,0:T(8,128)(2,1)}, bf16[8,32,896]{2,1,0:T(8,128)(2,1)}) custom-call(bf16[256,1024]{1,0:T(8,128)(2,1)} %get-tuple-element.6.mixed, f32[8,256]{1,0:T(8,128)} %get-tuple-element.7.squares, bf16[8,32,896]{2,1,0:T(8,128)(2,1)} %get-tuple-element.8.rows, bf16[8,32,896]{2,1,0:T(8,128)(2,1)} %enc.3, ...), custom_call_target="tpu_custom_call" | custom-call | tf_op jit(solution)/shard_map/finish/pallas_call | solution.py:490

commit v3 on v2

--- a/solution.py
+++ b/solution.py
@@ -22,6 +22,10 @@
 
 def rms_scale(values):
     return lax.rsqrt(jnp.mean(values * values, axis=-1, keepdims=True) + EPS)
+
+
+def row_of(gain):
+    return jnp.concatenate([gain[i : i + 1] for i in range(gain.shape[0])], axis=1)
 
 
 def place(n_dp, n_mp):
@@ -59,6 +63,8 @@
     head_cols = wq.shape[2]
     heads = head_cols // HD
     factor = HD ** (-0.5)
+    cut = width // 256 * 128
+    spans = (slice(0, cut), slice(cut, width), slice(0, feat))
     loads = [
         pltpu.make_async_copy(a, b, w_sem.at[i])
         for i, (a, b) in enumerate([(wq_hbm, wq), (wo_hbm, wo), (wk_hbm, wk), (wv_hbm, wv)])
@@ -110,20 +116,25 @@
     def row_copy(s, src, dst):
         return dp_copy(sending.at[src], arrived.at[dst], row_send, row_recv, s)
 
-    def back_copy(s, src, dst):
-        return dp_copy(back_out.at[src], back_in.at[dst], back_send, back_recv, s)
+    def back_copy(t, s, src, dst):
+        cols = spans[t]
+        return dp_copy(
+            back_out.at[src, :, cols], back_in.at[dst, :, cols],
+            back_send.at[t], back_recv.at[t], s,
+        )
 
     def near(buf, land, t, i):
+        cols = spans[t]
         return pltpu.make_async_remote_copy(
-            src_ref=buf.at[i * 2 + 1 - c], dst_ref=land.at[i],
+            src_ref=buf.at[i * 2 + 1 - c, ..., cols], dst_ref=land.at[i, ..., cols],
             send_sem=near_send.at[t, i], recv_sem=near_recv.at[t, i],
             device_id=(d, partner), device_id_type=MESH,
         )
 
     def far(buf, land, t, o):
-        to = (x + o) % n_x
+        to, cols = (x + o) % n_x, spans[t]
         return pltpu.make_async_remote_copy(
-            src_ref=buf.at[to], dst_ref=land.at[o],
+            src_ref=buf.at[to, ..., cols], dst_ref=land.at[o, ..., cols],
             send_sem=far_send.at[t, o], recv_sem=far_recv.at[t, o],
             device_id=(d, to * 2 + c), device_id_type=MESH,
         )
@@ -135,14 +146,15 @@
         )
 
     def pair_up(buf, land, pair, t):
-        for i in range(n_x):
-            near(buf, land, t, i).wait_recv()
+        cols = spans[t]
         for o in range(1, n_x):
             to = (x + o) % n_x
-            pair[to] = (buf[to * 2 + c].astype(F32) + land[to].astype(F32)).astype(BF16)
+            near(buf, land, t, to).wait_recv()
+            theirs = land[to, ..., cols].astype(F32)
+            pair[to, ..., cols] = (buf[to * 2 + c, ..., cols].astype(F32) + theirs).astype(BF16)
 
     tok_all[m] = tok[...]
-    picks = [chosen[a // NEIGH, a % NEIGH] for a in range(readings)]
+    picks = [chosen[a % NEIGH, a // NEIGH] for a in range(readings)]
     spot = lax.broadcasted_iota(jnp.int32, (readings, 128), 0)
     listed = jnp.zeros((readings, 128), jnp.int32)
     for a in range(readings):
@@ -156,7 +168,7 @@
     cot_a[m] = cot[:half]
     cot_b[m] = cot[half:]
     wide = enc[...].astype(F32)
-    enc_norm[...] = wide * rms_scale(wide) * gain_enc[...][None]
+    enc_norm[...] = wide * rms_scale(wide) * row_of(gain_enc)[None]
 
     def choose(reader):
         asked = idtab[reader]
@@ -213,21 +225,32 @@
     forward(cot_a, 1)
     sent_far(enc_all, 3)
     spread(cot_b, 2)
-    forward(enc_all, 3)
-    finish(enc_all, 3)
     loads[2].wait()
     loads[3].wait()
 
-    def memory_tile(n, _):
-        cols = pl.ds(pl.multiple_of(n * 256, 256), 256)
-        for k in range(n_mp):
-            rows = enc_all[k].reshape(readings * share, width)
+    def project_memory(k):
+        toks = pl.ds(pl.multiple_of(k * share, share), share)
+        rows = enc_all[k].reshape(readings * share, width)
+
+        def tile(n, _):
+            cols = pl.ds(pl.multiple_of(n * 256, 256), 256)
             for weight, out in ((wk, keys), (wv, values)):
                 part = jnp.dot(rows, weight[:, cols], preferred_element_type=F32).astype(BF16)
-                out[:, k * share : (k + 1) * share, cols] = part.reshape(readings, share, 256)
-        return 0
-
-    lax.fori_loop(0, head_cols // 256, memory_tile, 0)
+                out[:, toks, cols] = part.reshape(readings, share, 256)
+            return 0
+
+        lax.fori_loop(0, head_cols // 256, tile, 0)
+
+    project_memory(m)
+    hop(enc_all, 3, 0, partner, partner).wait_recv()
+    project_memory(partner)
+    forward(enc_all, 3)
+    for o in range(1, n_x):
+        project_memory(((x + n_x - o) % n_x) * 2 + c)
+    for o in range(1, n_x):
+        chunk = ((x + n_x - o) % n_x) * 2 + 1 - c
+        hop(enc_all, 3, n_x + o, chunk, partner).wait_recv()
+        project_memory(chunk)
 
     def memory_of(buf, b, h):
         part = buf[pl.ds(b * NEIGH, NEIGH), :, h * HD : (h + 1) * HD]
@@ -235,8 +258,8 @@
 
     def attend(b, _):
         rows = pl.ds(pl.multiple_of(b * BLOCK, BLOCK), BLOCK)
-        for h0 in range(0, heads, 4):
-            group = range(h0, h0 + 4)
+        for h0 in range(0, heads, 8):
+            group = range(h0, min(h0 + 8, heads))
             scores = [
                 lax.dot_general(
                     q[rows, h * HD : (h + 1) * HD], memory_of(keys, b, h), NT,
@@ -266,11 +289,11 @@
 
     lax.fori_loop(0, n_mp, branch_chunk, 0)
     for i in range(n_x):
-        near(branches, b_near, 1, i).start()
+        near(branches, b_near, 2, i).start()
     forward(cot_b, 2)
-    pair_up(branches, b_near, b_pair, 1)
-    for o in range(1, n_x):
-        far(b_pair, b_far, 1, o).start()
+    pair_up(branches, b_near, b_pair, 2)
+    for o in range(1, n_x):
+        far(b_pair, b_far, 2, o).start()
     finish(cot_a, 1)
     finish(cot_b, 2)
 
@@ -290,8 +313,8 @@
     def attend_back(b, _):
         rows = pl.ds(pl.multiple_of(b * BLOCK, BLOCK), BLOCK)
         mem = pl.ds(b * NEIGH, NEIGH)
-        for h0 in range(0, heads, 4):
-            group = range(h0, h0 + 4)
+        for h0 in range(0, heads, 8):
+            group = range(h0, min(h0 + 8, heads))
             d_prob = [
                 lax.dot_general(
                     da[rows, h * HD : (h + 1) * HD], memory_of(values, b, h), NT,
@@ -318,35 +341,44 @@
 
     lax.fori_loop(0, seq_len // BLOCK, attend_back, 0)
 
-    def enc_chunk(k):
+    def enc_chunk(k, t):
         toks = pl.ds(pl.multiple_of(k * share, share), share)
+        cols = spans[t]
         acc = lax.dot_general(
-            dk[:, toks, :].reshape(readings * share, head_cols), wk[...], NT,
+            dk[:, toks, :].reshape(readings * share, head_cols), wk[cols, :], NT,
             preferred_element_type=F32,
         )
         acc += lax.dot_general(
-            dv[:, toks, :].reshape(readings * share, head_cols), wv[...], NT,
+            dv[:, toks, :].reshape(readings * share, head_cols), wv[cols, :], NT,
             preferred_element_type=F32,
         )
-        enc_terms[k] = acc.astype(BF16).reshape(readings, share, width)
-
-    def partner_chunk(i, _):
-        enc_chunk(i * 2 + 1 - c)
-        near(enc_terms, e_near, 0, i).start()
-        return 0
-
-    def own_chunk(i, _):
-        enc_chunk(i * 2 + c)
-        return 0
-
-    lax.fori_loop(0, n_x, partner_chunk, 0)
-    lax.fori_loop(0, n_x, own_chunk, 0)
-    pair_up(enc_terms, e_near, e_pair, 0)
-    for o in range(1, n_x):
-        far(e_pair, e_far, 0, o).start()
+        enc_terms[k, :, :, cols] = acc.astype(BF16).reshape(readings, share, cols.stop - cols.start)
+
+    for t in range(2):
+        for o in range(1, n_x):
+            to = (x + o) % n_x
+            enc_chunk(to * 2 + 1 - c, t)
+            near(enc_terms, e_near, t, to).start()
+        for o in range(1, n_x):
+            enc_chunk((x + o) % n_x * 2 + c, t)
+        if t == 0:
+            pair_up(enc_terms, e_near, e_pair, 0)
+            for o in range(1, n_x):
+                far(e_pair, e_far, 0, o).start()
+    pair_up(enc_terms, e_near, e_pair, 1)
+    for t in range(2):
+        enc_chunk(x * 2 + 1 - c, t)
+        near(enc_terms, e_near, t, x).start()
+    for t in range(2):
+        enc_chunk(x * 2 + c, t)
+    for o in range(1, n_x):
+        far(e_pair, e_far, 0, o).wait_send()
+    for o in range(1, n_x):
+        far(e_pair, e_far, 1, o).start()
+    near(branches, b_near, 2, x).wait_recv()
     added = branches[m].astype(F32) + b_near[x].astype(F32)
     for o in range(1, n_x):
-        far(b_pair, b_far, 1, o).wait_recv()
+        far(b_pair, b_far, 2, o).wait_recv()
         added = added + b_far[o].astype(F32)
     mixed = (tok[...].astype(F32) + added).astype(BF16)
     mixed_out[...] = mixed
@@ -355,23 +387,26 @@
     sq_mine[...] = jnp.transpose(squares)[:8]
     for s in range(1, n_mp):
         sq_copy(s).start()
-    total = enc_terms[m].astype(F32) + e_near[x].astype(F32)
-    for o in range(1, n_x):
-        far(e_pair, e_far, 0, o).wait_recv()
-        total = total + e_far[o].astype(F32)
-    d_norm[...] = total.astype(BF16)
-
     def reading_of(holder):
         found = jnp.int32(0)
         for a in range(readings):
             found = jnp.where(picks[a] // own_rows == holder, a, found)
         return found
 
-    for s in range(1, n_dp):
-        holder = (d + s) % n_dp
-        back_out[holder] = d_norm[reading_of(holder)]
-        back_copy(s, holder, d).start()
-    back_in[d] = d_norm[reading_of(d)]
+    finders = [reading_of((d + s) % n_dp) for s in range(n_dp)]
+    for t in range(2):
+        cols = spans[t]
+        near(enc_terms, e_near, t, x).wait_recv()
+        total = enc_terms[m, :, :, cols].astype(F32) + e_near[x, :, :, cols].astype(F32)
+        for o in range(1, n_x):
+            far(e_pair, e_far, t, o).wait_recv()
+            total = total + e_far[o, :, :, cols].astype(F32)
+        d_norm[:, :, cols] = total.astype(BF16)
+        for s in range(1, n_dp):
+            holder = (d + s) % n_dp
+            back_out[holder, :, cols] = d_norm[finders[s], :, cols]
+            back_copy(t, s, holder, d).start()
+    back_in[d] = d_norm[finders[0]]
     squares = sq_mine[...]
     for s in range(1, n_mp):
         sq_copy(s).wait_recv()
@@ -379,25 +414,27 @@
     squares_out[...] = squares
     for s in range(1, n_dp):
         source = (d + n_dp - s) % n_dp
-        back_copy(s, source, source).wait_recv()
+        for t in range(2):
+            back_copy(t, s, source, source).wait_recv()
     for row in range(own_rows):
         rows_out[row] = back_in[askers[row]]
     sent_far(cot_a, 1)
     sent_far(cot_b, 2)
     for t, buf in enumerate((tok_all, cot_a, cot_b, enc_all)):
         sent_near(buf, t)
-    for t, (buf, land, pair, beyond) in enumerate(
-        ((enc_terms, e_near, e_pair, e_far), (branches, b_near, b_pair, b_far))
-    ):
-        for i in range(n_x):
-            near(buf, land, t, i).wait_send()
-        for o in range(1, n_x):
-            far(pair, beyond, t, o).wait_send()
+    for i in range(n_x):
+        for t in range(2):
+            near(enc_terms, e_near, t, i).wait_send()
+        near(branches, b_near, 2, i).wait_send()
+    for o in range(1, n_x):
+        far(e_pair, e_far, 1, o).wait_send()
+        far(b_pair, b_far, 2, o).wait_send()
     for s in range(1, n_dp):
         to = (d + s) % n_dp
         id_copy(s, d).wait_send()
         row_copy(s, to, d).wait_send()
-        back_copy(s, to, d).wait_send()
+        for t in range(2):
+            back_copy(t, s, to, d).wait_send()
     for s in range(1, n_mp):
         sq_copy(s).wait_send()
 
@@ -405,6 +442,7 @@
 def finish_kernel(n_mp, mixed, squares, rows, enc, gain_enc, gain_post, mixed_out, ffn_out, denc_out):
     seq_len, feat = mixed.shape
     mixed_out[...] = mixed[...]
+    gain_row = row_of(gain_enc)
     scale = jnp.transpose(jnp.broadcast_to(squares[:1], (128, seq_len)))[:, :1]
     scale = lax.rsqrt(scale / (feat * n_mp) + EPS)
     gain = gain_post[lax.axis_index("mp")]
@@ -413,7 +451,7 @@
         wide = enc[row].astype(F32)
         scale = rms_scale(wide)
         hat = wide * scale
-        up = gain_enc[...] * rows[row].astype(F32)
+        up = gain_row * rows[row].astype(F32)
         inner = jnp.mean(up * hat, axis=-1, keepdims=True)
         denc_out[row] = (scale * (up - hat * inner)).astype(BF16)
 
@@ -435,7 +473,7 @@
     dma = pltpu.SemaphoreType.DMA
     shape = jax.ShapeDtypeStruct
     vmem = pltpu.VMEM
-    gain_enc = gain_enc.reshape(1, width)
+    gain_enc = gain_enc.reshape(width // 128, 128)
     tokens_all = vmem((n_mp, seq_len, feat), BF16)
     half_all = vmem((n_mp, seq_len // 2, feat), BF16)
     rows_all = vmem((n_mp, readings, share, width), BF16)
@@ -476,8 +514,8 @@
             dma((4,)),
             dma((4, 2 * n_x)), dma((4, 2 * n_x)),
             dma((n_dp,)), dma((n_dp,)), dma((n_dp,)), dma((n_dp,)),
-            dma((2, n_x)), dma((2, n_x)), dma((2, n_x)), dma((2, n_x)),
-            dma((n_dp,)), dma((n_dp,)), dma((n_mp,)), dma((n_mp,)),
+            dma((3, n_x)), dma((3, n_x)), dma((3, n_x)), dma((3, n_x)),
+            dma((2, n_dp)), dma((2, n_dp)), dma((n_mp,)), dma((n_mp,)),
         ],
         compiler_params=pltpu.CompilerParams(
             collective_id=0, has_side_effects=True, vmem_limit_bytes=60 * 1024 * 1024
@@ -485,7 +523,7 @@
         name="layer",
     )(
         tokens, cotangent, gain_dec.reshape(n_mp, 1, feat), w_query.reshape(n_mp, feat, head_cols),
-        w_out, encodings, gain_enc, w_key, w_value, neighbour_ids,
+        w_out, encodings, gain_enc, w_key, w_value, neighbour_ids.T,
     )
     return pl.pallas_call(
         functools.partial(finish_kernel, n_mp),

time: 91.8 us -> 84.3 us (0.918)
  Pallas kernels: 88 us -> 83.5 us
  local copies, waits for them, and re-layouts: 2.62 us -> 0 us
    pallas_call x1, Pallas kernels: 85 us -> 80.5 us  [shards(): pl.pallas_call(functools.partial(layer_kernel, n_dp, n_mp), out_shape=(sh...]
    unnamed x1 -> x0, local copies, waits for them, and re-layouts: 1.34 us -> none
    reshape x1 -> x0, local copies, waits for them, and re-layouts: 1.28 us -> none  [shards(): gain_enc = gain_enc.reshape(1, width)]
where the time goes in v3:
time: 84.3 us; the launch traced here: 84.1 us
  Pallas kernels  83.5 us (99%)
    pallas_call x1, Pallas kernels, shards(): pl.pallas_call(functools.partial(layer_kernel, n_dp, n_mp), out_shape=(sh...  80.5 us
    pallas_call x1, Pallas kernels, shards(): pl.pallas_call(functools.partial(finish_kernel, n_mp), out_shape=(shape((...  2.94 us

profile of v3, /device:TPU:0, one launch (start us, length us, event | category | flops | bytes accessed | tf_op | source)
XLA Modules:
  0.0 84.1 jit_solution(3621731028357180580)
XLA Ops:
  0.6 80.5 %layer.1 = (bf16[256,1024]{1,0:T(8,128)(2,1)}, f32[8,256]{1,0:T(8,128)}, bf16[8,32,896]{2,1,0:T(8,128)(2,1)}) custom-call(bf16[256,1024]{1,0:T(8,128)(2,1)} %tok.1, bf16[256,1024]{1,0:T(8,128)(2,1)} %cot.1, f32[4,1,1024]{2,1,0:T(1,128)} %bitcast.7, bf16[4,1024,1024]{2,1,0:T(8,128)(2,1)} %bitcast.5, bf16[1024,4096]{1,0:T(8,128)(2,1)} %wo_hbm.1, ...), custom_call_target="tpu_custom_call" | custom-call | tf_op jit(solution)/shard_map/layer/pallas_call | solution.py:485
  81.2 2.9 %finish.1 = (bf16[256,1024]{1,0:T(8,128)(2,1)}, bf16[256,1024]{1,0:T(8,128)(2,1)}, bf16[8,32,896]{2,1,0:T(8,128)(2,1)}) custom-call(bf16[256,1024]{1,0:T(8,128)(2,1)} %get-tuple-element.6.mixed, f32[8,256]{1,0:T(8,128)} %get-tuple-element.7.squares, bf16[8,32,896]{2,1,0:T(8,128)(2,1)} %get-tuple-element.8.rows, bf16[8,32,896]{2,1,0:T(8,128)(2,1)} %enc.3, ...), custom_call_target="tpu_custom_call" | custom-call | tf_op jit(solution)/shard_map/finish/pallas_call | solution.py:528

commit v4 on v3

--- a/solution.py
+++ b/solution.py
@@ -12,6 +12,7 @@
 NLEN = 128
 NEIGH = 2
 LEAD = BLOCK - 1
+LOG2_E = 1.4426950408889634
 EPS = 1e-06
 MESH = pl.DeviceIdType.MESH
 BF16 = jnp.bfloat16
@@ -63,12 +64,24 @@
     head_cols = wq.shape[2]
     heads = head_cols // HD
     factor = HD ** (-0.5)
-    cut = width // 256 * 128
+    cut = (width + 128) // 256 * 128
     spans = (slice(0, cut), slice(cut, width), slice(0, feat))
     loads = [
         pltpu.make_async_copy(a, b, w_sem.at[i])
         for i, (a, b) in enumerate([(wq_hbm, wq), (wo_hbm, wo), (wk_hbm, wk), (wv_hbm, wv)])
     ]
+    own = [
+        pltpu.make_async_copy(a, b, w_sem.at[4 + i])
+        for i, (a, b) in enumerate(
+            [
+                (tok, tok_all.at[m]),
+                (cot.at[pl.ds(0, half)], cot_a.at[m]),
+                (cot.at[pl.ds(half, half)], cot_b.at[m]),
+            ]
+        )
+    ]
+    for copy in own:
+        copy.start()
     for i in (0, 2, 3, 1):
         loads[i].start()
 
@@ -153,7 +166,6 @@
             theirs = land[to, ..., cols].astype(F32)
             pair[to, ..., cols] = (buf[to * 2 + c, ..., cols].astype(F32) + theirs).astype(BF16)
 
-    tok_all[m] = tok[...]
     picks = [chosen[a % NEIGH, a // NEIGH] for a in range(readings)]
     spot = lax.broadcasted_iota(jnp.int32, (readings, 128), 0)
     listed = jnp.zeros((readings, 128), jnp.int32)
@@ -163,10 +175,9 @@
     greet(n_dp, n_mp, d, m)
     for s in range(1, n_dp):
         id_copy(s, d).start()
+    own[0].wait()
     spread(tok_all, 0)
     idtab[d] = listed
-    cot_a[m] = cot[:half]
-    cot_b[m] = cot[half:]
     wide = enc[...].astype(F32)
     enc_norm[...] = wide * rms_scale(wide) * row_of(gain_enc)[None]
 
@@ -186,6 +197,7 @@
         row_copy(s, reader, d).start()
     arrived[d] = choose(d)
     sent_far(tok_all, 0)
+    own[1].wait()
     spread(cot_a, 1)
     forward(tok_all, 0)
     table = idtab[...]
@@ -224,6 +236,7 @@
     lax.fori_loop(0, head_cols // 256, query_tile, 0)
     forward(cot_a, 1)
     sent_far(enc_all, 3)
+    own[2].wait()
     spread(cot_b, 2)
     loads[2].wait()
     loads[3].wait()
@@ -264,11 +277,13 @@
                 lax.dot_general(
                     q[rows, h * HD : (h + 1) * HD], memory_of(keys, b, h), NT,
                     preferred_element_type=F32,
-                ) * factor
+                )
                 for h in group
             ]
-            lifted = [jnp.exp(v - jnp.max(v, axis=-1, keepdims=True)) for v in scores]
-            prob = [v / jnp.sum(v, axis=-1, keepdims=True) for v in lifted]
+            lifted = [
+                jnp.exp2((v - jnp.max(v, axis=-1, keepdims=True)) * (factor * LOG2_E)) for v in scores
+            ]
+            prob = [v * (1.0 / jnp.sum(v, axis=-1, keepdims=True)) for v in lifted]
             for h, v in zip(group, prob):
                 prob_all[b, h] = v
             for h, v in zip(group, prob):
@@ -380,7 +395,7 @@
     for o in range(1, n_x):
         far(b_pair, b_far, 2, o).wait_recv()
         added = added + b_far[o].astype(F32)
-    mixed = (tok[...].astype(F32) + added).astype(BF16)
+    mixed = (tok_all[m].astype(F32) + added).astype(BF16)
     mixed_out[...] = mixed
     wide = mixed.astype(F32)
     squares = jnp.broadcast_to(jnp.sum(wide * wide, axis=-1, keepdims=True), (seq_len, 128))
@@ -489,7 +504,7 @@
             shape((8, seq_len), F32),
             shape((own_rows, share, width), BF16),
         ),
-        in_specs=[block] * 3 + [anywhere] * 2 + [block] * 2 + [anywhere] * 2 + [smem],
+        in_specs=[anywhere] * 2 + [block] + [anywhere] * 2 + [block] * 2 + [anywhere] * 2 + [smem],
         out_specs=(block,) * 3,
         scratch_shapes=[
             tokens_all, half_all, half_all, rows_all, tokens_all,
@@ -511,7 +526,7 @@
             slots, slots,
             vmem((8, seq_len), F32),
             vmem((n_mp, 8, seq_len), F32),
-            dma((4,)),
+            dma((7,)),
             dma((4, 2 * n_x)), dma((4, 2 * n_x)),
             dma((n_dp,)), dma((n_dp,)), dma((n_dp,)), dma((n_dp,)),
             dma((3, n_x)), dma((3, n_x)), dma((3, n_x)), dma((3, n_x)),

time: 84.3 us -> 85 us (level)
  no operation moved by 1% of the time
where the time goes in v4:
time: 85 us; the launch traced here: 84.8 us
  Pallas kernels  84.2 us (99%)
    pallas_call x1, Pallas kernels, shards(): pl.pallas_call(functools.partial(layer_kernel, n_dp, n_mp), out_shape=(sh...  81.2 us
    pallas_call x1, Pallas kernels, shards(): pl.pallas_call(functools.partial(finish_kernel, n_mp), out_shape=(shape((...  2.94 us

profile of v4, /device:TPU:0, one launch (start us, length us, event | category | flops | bytes accessed | tf_op | source)
XLA Modules:
  0.0 84.8 jit_solution(16658748922261640401)
XLA Ops:
  0.6 81.2 %layer.1 = (bf16[256,1024]{1,0:T(8,128)(2,1)}, f32[8,256]{1,0:T(8,128)}, bf16[8,32,896]{2,1,0:T(8,128)(2,1)}) custom-call(bf16[256,1024]{1,0:T(8,128)(2,1)} %tok.1, bf16[256,1024]{1,0:T(8,128)(2,1)} %cot.1, f32[4,1,1024]{2,1,0:T(1,128)} %bitcast.7, bf16[4,1024,1024]{2,1,0:T(8,128)(2,1)} %bitcast.5, bf16[1024,4096]{1,0:T(8,128)(2,1)} %wo_hbm.1, ...), custom_call_target="tpu_custom_call" | custom-call | tf_op jit(solution)/shard_map/layer/pallas_call | solution.py:500
  81.9 2.9 %finish.1 = (bf16[256,1024]{1,0:T(8,128)(2,1)}, bf16[256,1024]{1,0:T(8,128)(2,1)}, bf16[8,32,896]{2,1,0:T(8,128)(2,1)}) custom-call(bf16[256,1024]{1,0:T(8,128)(2,1)} %get-tuple-element.6.mixed, f32[8,256]{1,0:T(8,128)} %get-tuple-element.7.squares, bf16[8,32,896]{2,1,0:T(8,128)(2,1)} %get-tuple-element.8.rows, bf16[8,32,896]{2,1,0:T(8,128)(2,1)} %enc.3, ...), custom_call_target="tpu_custom_call" | custom-call | tf_op jit(solution)/shard_map/finish/pallas_call | solution.py:543

commit v5 on v4

--- a/solution.py
+++ b/solution.py
@@ -64,7 +64,7 @@
     head_cols = wq.shape[2]
     heads = head_cols // HD
     factor = HD ** (-0.5)
-    cut = (width + 128) // 256 * 128
+    cut = width // 256 * 128
     spans = (slice(0, cut), slice(cut, width), slice(0, feat))
     loads = [
         pltpu.make_async_copy(a, b, w_sem.at[i])
@@ -197,8 +197,6 @@
         row_copy(s, reader, d).start()
     arrived[d] = choose(d)
     sent_far(tok_all, 0)
-    own[1].wait()
-    spread(cot_a, 1)
     forward(tok_all, 0)
     table = idtab[...]
     owner_at = lax.broadcasted_iota(jnp.int32, table.shape, 0)
@@ -234,8 +232,9 @@
         return 0
 
     lax.fori_loop(0, head_cols // 256, query_tile, 0)
-    forward(cot_a, 1)
     sent_far(enc_all, 3)
+    own[1].wait()
+    spread(cot_a, 1)
     own[2].wait()
     spread(cot_b, 2)
     loads[2].wait()
@@ -264,6 +263,7 @@
         chunk = ((x + n_x - o) % n_x) * 2 + 1 - c
         hop(enc_all, 3, n_x + o, chunk, partner).wait_recv()
         project_memory(chunk)
+    forward(cot_a, 1)
 
     def memory_of(buf, b, h):
         part = buf[pl.ds(b * NEIGH, NEIGH), :, h * HD : (h + 1) * HD]

time: 85 us -> 81.4 us (0.958)
  Pallas kernels: 84.2 us -> 80.6 us
    pallas_call x1, Pallas kernels: 81.2 us -> 77.6 us  [shards(): pl.pallas_call(functools.partial(layer_kernel, n_dp, n_mp), out_shape=(sh...]
where the time goes in v5:
time: 81.4 us; the launch traced here: 81.2 us
  Pallas kernels  80.6 us (99%)
    pallas_call x1, Pallas kernels, shards(): pl.pallas_call(functools.partial(layer_kernel, n_dp, n_mp), out_shape=(sh...  77.6 us
    pallas_call x1, Pallas kernels, shards(): pl.pallas_call(functools.partial(finish_kernel, n_mp), out_shape=(shape((...  2.94 us

profile of v5, /device:TPU:0, one launch (start us, length us, event | category | flops | bytes accessed | tf_op | source)
XLA Modules:
  0.0 81.2 jit_solution(5967346939259703389)
XLA Ops:
  0.6 77.6 %layer.1 = (bf16[256,1024]{1,0:T(8,128)(2,1)}, f32[8,256]{1,0:T(8,128)}, bf16[8,32,896]{2,1,0:T(8,128)(2,1)}) custom-call(bf16[256,1024]{1,0:T(8,128)(2,1)} %tok.1, bf16[256,1024]{1,0:T(8,128)(2,1)} %cot.1, f32[4,1,1024]{2,1,0:T(1,128)} %bitcast.7, bf16[4,1024,1024]{2,1,0:T(8,128)(2,1)} %bitcast.5, bf16[1024,4096]{1,0:T(8,128)(2,1)} %wo_hbm.1, ...), custom_call_target="tpu_custom_call" | custom-call | tf_op jit(solution)/shard_map/layer/pallas_call | solution.py:500
  78.3 2.9 %finish.1 = (bf16[256,1024]{1,0:T(8,128)(2,1)}, bf16[256,1024]{1,0:T(8,128)(2,1)}, bf16[8,32,896]{2,1,0:T(8,128)(2,1)}) custom-call(bf16[256,1024]{1,0:T(8,128)(2,1)} %get-tuple-element.6.mixed, f32[8,256]{1,0:T(8,128)} %get-tuple-element.7.squares, bf16[8,32,896]{2,1,0:T(8,128)(2,1)} %get-tuple-element.8.rows, bf16[8,32,896]{2,1,0:T(8,128)(2,1)} %enc.3, ...), custom_call_target="tpu_custom_call" | custom-call | tf_op jit(solution)/shard_map/finish/pallas_call | solution.py:543
